TPU v7x, 512 devices: a whole 4x8x8 slice. The times are simulated.
512 devices in a mesh: seq: 32 (over z, y_hi, core), vocab: 16 (over y_lo, x).
Axes of the slice: x: 4, y: 8 (y_hi: 2, y_lo: 4; y = y_hi * 4 + y_lo), z: 8, core: 2. Of those that a mesh axis runs over, the one named last changes fastest.
Arguments:
- hidden: bfloat16 [4096, 4096], P('seq', 'vocab'), may hold values from -14 to 14
- head_weight: bfloat16 [2, 4096, 4096], P(None, None, 'vocab'), may hold values from -0.09375 to 0.09375
- gains: bfloat16 [2, 4096], P(None, 'vocab'), may hold values from 0.099609375 to 1.8984375
- unembed: bfloat16 [4096, 16384], P('seq', 'vocab'), may hold values from -3.5 to 3.5
- targets: int32 [2, 4096], P(None, 'seq'), may hold values from 0 to 16383
- loss_weights: float32 [2], replicated, may hold values from 2 to 8
Outputs:
- losses: float32 [2], replicated
- input_grad: float32 [4096, 4096], P('seq', 'vocab')
- gain_grad: float32 [2, 4096], P(None, 'vocab')
All inputs are finite; a program needn't handle non-finite values.
Results may differ from a plain program's by a relative error of at most 0.02.
The roundings to bfloat16 on the way count: a program that leaves them out, or rounds other values in their place, can miss the bound.
Values may be sent and summed in bfloat16 or wider, within the bound.
A program may use at most 64 MiB of HBM per device.

v0:
```python
import jax
import jax.numpy as jnp
from jax import lax
from jax.sharding import PartitionSpec as P

eps = 1e-05


def per_device(hidden, head_weight, gains, unembed, targets, loss_weights):
    rows = hidden.shape[0]
    cols = hidden.shape[1]
    vocab_dev = unembed.shape[1]
    full, gain_full = (
        lax.all_gather(hidden, "vocab", axis=1, tiled=True),
        lax.all_gather(gains, "vocab", axis=1, tiled=True),
    )
    table = None
    table = lax.all_gather(unembed, "seq", axis=0, tiled=True)
    x = full.astype(jnp.float32)
    width = x.shape[1]
    r = lax.rsqrt(jnp.mean(x * x, axis=-1, keepdims=True) + eps)
    x_cols = hidden.astype(jnp.float32)
    x_trans = x_cols.T
    r_trans = r.T
    offset = lax.axis_index("vocab") * vocab_dev
    column_ids = lax.broadcasted_iota(jnp.int32, (1, vocab_dev), 1) + offset
    total_trans = jnp.zeros((cols, rows), jnp.float32)
    count = head_weight.shape[0]
    loss_done = []
    gain_done = []
    for head in range(count):
        gain_row = gain_full[head].astype(jnp.float32)[None, :]
        normed = (x * r * gain_row).astype(jnp.bfloat16)
        branch = jnp.dot(normed, head_weight[head], preferred_element_type=jnp.float32)
        head_cols = (x_cols + branch).astype(jnp.bfloat16)
        head_full = lax.all_gather(head_cols, "vocab", axis=1, tiled=True)
        logits = jnp.dot(head_full, table, preferred_element_type=jnp.float32)
        picked = column_ids == targets[head][:, None]
        target_part = jnp.sum(jnp.where(picked, logits, 0.0), axis=-1)
        local_max = jnp.max(logits, axis=-1)
        top = lax.pmax(local_max, "vocab")
        total, target_logit = lax.psum(
            (jnp.sum(jnp.exp(logits - top[:, None]), axis=-1), target_part), "vocab"
        )
        lse = top + jnp.log(total)
        loss_part = jnp.sum(lse - target_logit)
        probs = jnp.exp(logits - lse[:, None])
        upstream = (loss_weights[head] * (probs - picked.astype(jnp.float32))).astype(jnp.bfloat16)
        head_grad = lax.psum_scatter(
            lax.dot_general(
                table, upstream, (((1,), (1,)), ((), ())), preferred_element_type=jnp.float32
            ).astype(jnp.bfloat16),
            "vocab",
            scatter_dimension=0,
            tiled=True,
        ).astype(jnp.float32)
        head_grad_low = head_grad.astype(jnp.bfloat16)
        weight = head_weight[head]
        norm_grad = lax.psum_scatter(
            jnp.dot(weight, head_grad_low, preferred_element_type=jnp.float32).astype(jnp.bfloat16),
            "vocab",
            scatter_dimension=0,
            tiled=True,
        ).astype(jnp.float32)
        gain_col = gains[head].astype(jnp.float32)[:, None]
        scaled = gain_col * norm_grad
        dots = lax.psum(jnp.sum(scaled * x_trans, axis=0), "vocab")
        input_part = (
            r_trans * scaled - x_trans * r_trans * r_trans * r_trans * dots[None, :] / width
        )
        total_trans = total_trans + head_grad + input_part
        gain_part = jnp.sum(norm_grad * x_trans * r_trans, axis=1)
        loss_sum, gain_sum = lax.psum((loss_part, gain_part), "seq")
        loss_done.append(loss_sum)
        gain_done.append(gain_sum)
    loss_all = jnp.stack(loss_done)
    gain_all = jnp.stack(gain_done)
    token_total = rows * lax.axis_size("seq")
    return (loss_all / token_total, total_trans.T, gain_all)


def solution(mesh):
    in_specs = (
        P("seq", "vocab"),
        P(None, None, "vocab"),
        P(None, "vocab"),
        P("seq", "vocab"),
        P(None, "seq"),
        P(),
    )
    out_specs = (P(), P("seq", "vocab"), P(None, "vocab"))
    return jax.shard_map(
        per_device, mesh=mesh, in_specs=in_specs, out_specs=out_specs, check_vma=False
    )
```

profile of v0, /device:TPU:56, one launch (start us, length us, event | category | flops | bytes accessed | tf_op | source)
XLA Modules:
  0.0 927.8 jit_solution(10366924281773803109)
XLA Ops:
  7.9 33.4 %all_gather.16 = bf16[2,4096]{1,0:T(2,128)(2,1)S(1)} all-gather(bf16[2,256]{1,0:T(2,128)(2,1)} %param.8), channel_id=1, replica_groups=mesh['seq'=32,'vocab'=16] {'vocab'}, dimensions={1}, use_global_device_ids=true | all-gather | bytes 17408 | tf_op jit(solution)/shard_map/all_gather | solution.py:15
  41.4 43.5 %all-gather.5.cloned.1.call-done = bf16[128,4096]{1,0:T(8,128)(2,1)} async-done(((bf16[128,256]{1,0:T(8,128)(2,1)}), bf16[128,4096]{1,0:T(8,128)(2,1)}) %all-gather.5.cloned.1.call-update) | async-done | bytes 1048592 | tf_op jit(solution)/shard_map/all_gather | solution.py:14
  84.9 1.5 fusion.8
  86.5 3.1 fusion.28
  90.4 2.7 fusion.25
  93.8 65.6 %all-gather.7.cloned.1.call-done = bf16[128,4096]{1,0:T(8,128)(2,1)} async-done(((bf16[128,256]{1,0:T(8,128)(2,1)}), bf16[128,4096]{1,0:T(8,128)(2,1)}) %all-gather.7.cloned.1.call-update) | async-done | bytes 1048592 | tf_op jit(solution)/shard_map/all_gather | solution.py:36
  159.4 127.9 %all-gather.9.cloned.1.call-done = bf16[4096,1024]{1,0:T(8,128)(2,1)} async-done(((bf16[128,1024]{1,0:T(8,128)(2,1)}), bf16[4096,1024]{1,0:T(8,128)(2,1)}) %all-gather.9.cloned.1.call-update) | async-done | bytes 8388624 | tf_op jit(solution)/shard_map/all_gather | solution.py:18
  287.3 5.0 fusion.82
  292.3 70.9 %all-gather.11.cloned.1.call-done = bf16[128,4096]{1,0:T(8,128)(2,1)} async-done(((bf16[128,256]{1,0:T(8,128)(2,1)}), bf16[128,4096]{1,0:T(8,128)(2,1)}) %all-gather.11.cloned.1.call-update) | async-done | bytes 1048592 | tf_op jit(solution)/shard_map/all_gather | solution.py:36
  363.2 5.0 fusion.81
  368.3 34.5 %all-reduce.3 = (f32[128]{0:T(128)S(1)}, f32[128]{0:T(128)S(1)}) all-reduce(f32[128]{0:T(128)S(1)} %get-tuple-element.35, f32[128]{0:T(128)S(1)} %get-tuple-element.37), channel_id=1, replica_groups=mesh['seq'=32,'vocab'=16] {'vocab'}, use_global_device_ids=true, to_apply=%region_10.11 | all-reduce | flops 256 | bytes 2048 | tf_op jit(solution)/shard_map/pmax | solution.py:41
  403.2 39.3 %all-reduce.2 = (f32[128]{0:T(128)S(1)}, f32[128]{0:T(128)S(1)}) all-reduce(f32[128]{0:T(128)S(1)} %get-tuple-element.13, f32[128]{0:T(128)S(1)} %get-tuple-element.4), channel_id=1, replica_groups=mesh['seq'=32,'vocab'=16] {'vocab'}, use_global_device_ids=true, to_apply=%region_12.13 | all-reduce | flops 256 | bytes 2048 | tf_op jit(solution)/shard_map/psum | solution.py:42
  442.6 8.0 fusion
  450.6 8.1 fusion.1
  458.8 77.9 %reduce-scatter.5.cloned.1.call-done = bf16[256,128]{0,1:T(8,128)(2,1)} async-done(((bf16[4096,128]{0,1:T(8,128)(2,1)}), bf16[256,128]{0,1:T(8,128)(2,1)}) %reduce-scatter.5.cloned.1.call-update) | async-done | bytes 65552 | tf_op jit(solution)/shard_map/reduce_scatter | solution.py:49
  536.7 3.4 fusion.2
  540.2 83.4 %reduce-scatter.9.cloned.1.call-done = bf16[256,128]{0,1:T(8,128)(2,1)} async-done(((bf16[4096,128]{0,1:T(8,128)(2,1)}), bf16[256,128]{0,1:T(8,128)(2,1)}) %reduce-scatter.9.cloned.1.call-update) | async-done | bytes 65552 | tf_op jit(solution)/shard_map/reduce_scatter | solution.py:49
  623.6 3.5 fusion.3
  627.2 83.5 %reduce-scatter.7.cloned.1.call-done = bf16[256,128]{0,1:T(8,128)(2,1)} async-done(((bf16[4096,128]{0,1:T(8,128)(2,1)}), bf16[256,128]{0,1:T(8,128)(2,1)}) %reduce-scatter.7.cloned.1.call-update) | async-done | bytes 65552 | tf_op jit(solution)/shard_map/reduce_scatter | solution.py:59
  710.7 87.2 %reduce-scatter.11.cloned.1.call-done = bf16[256,128]{0,1:T(8,128)(2,1)} async-done(((bf16[4096,128]{0,1:T(8,128)(2,1)}), bf16[256,128]{0,1:T(8,128)(2,1)}) %reduce-scatter.11.cloned.1.call-update) | async-done | bytes 65552 | tf_op jit(solution)/shard_map/reduce_scatter | solution.py:59
  798.9 39.2 %all-reduce.1 = (f32[128]{0:T(128)S(1)}, f32[128]{0:T(128)S(1)}, f32[128]{0:T(128)S(1)}, f32[128]{0:T(128)S(1)}) all-reduce(f32[128]{0:T(128)S(1)} %get-tuple-element.14, f32[128]{0:T(128)S(1)} %get-tuple-element.3, f32[128]{0:T(128)S(1)} %get-tuple-element.11, ...), channel_id=1, replica_groups=mesh['seq'=32,'vocab'=16] {'vocab'}, use_global_device_ids=true, to_apply=%region_14.15 | all-reduce | flops 512 | bytes 4096 | tf_op jit(solution)/shard_map/psum | solution.py:42
  838.7 78.1 %all-reduce = (f32[1]{0:T(128)}, f32[1]{0:T(128)}, f32[1,256]{1,0:T(1,128)S(1)}, f32[1,256]{1,0:T(1,128)S(1)}) all-reduce(f32[1]{0:T(128)} %bitcast.7, f32[1]{0:T(128)} %bitcast.3, f32[1,256]{1,0:T(1,128)S(1)} %bitcast.97, f32[1,256]{1,0:T(1,128)S(1)} %bitcast.96), channel_id=1, replica_groups=mesh['seq'=32,'vocab'=16] {'seq'}, use_global_device_ids=true, to_apply=%region_16.17 | all-reduce | flops 514 | bytes 4112 | tf_op jit(solution)/shard_map/psum | solution.py:73
  917.4 1.9 maximum_multiply_fusion
  919.3 1.7 fusion.64
  (42 shorter events, 5.1 us)
Async XLA Ops:
  7.2 77.8 %all-gather.5.cloned.1.call-start = ((), (), s32[]{:S(2)}) async-start(), calls=%async_computation.4 | async-start | bytes 1114112 | tf_op jit(solution)/shard_map/all_gather | solution.py:14
  7.9 151.5 %all-gather.7.cloned.1.call-start = ((), (), s32[]{:S(2)}) async-start(), calls=%async_computation.5 | async-start | bytes 1114112 | tf_op jit(solution)/shard_map/all_gather | solution.py:36
  86.5 3.9 copy-start
  86.5 3.9 copy-start.1
  89.6 197.7 %all-gather.9.cloned.1.call-start = ((), (), s32[]{:S(2)}) async-start(), calls=%async_computation.6 | async-start | bytes 8650752 | tf_op jit(solution)/shard_map/all_gather | solution.py:18
  90.3 272.9 %all-gather.11.cloned.1.call-start = ((), (), s32[]{:S(2)}) async-start(), calls=%async_computation.7 | async-start | bytes 1114112 | tf_op jit(solution)/shard_map/all_gather | solution.py:36
  90.4 2.8 copy-start.5
  90.4 3.4 copy-start.6
  93.1 443.5 %reduce-scatter.5.cloned.1.call-start = ((), (), s32[]{:S(2)}) async-start(), calls=%async_computation.8 | async-start | bytes 1114112 | tf_op jit(solution)/shard_map/reduce_scatter | solution.py:49
  450.5 173.1 %reduce-scatter.9.cloned.1.call-start = ((), (), s32[]{:S(2)}) async-start(), calls=%async_computation.10 | async-start | bytes 1114112 | tf_op jit(solution)/shard_map/reduce_scatter | solution.py:49
  458.7 252.0 %reduce-scatter.7.cloned.1.call-start = ((), (), s32[]{:S(2)}) async-start(), calls=%async_computation.9 | async-start | bytes 1114112 | tf_op jit(solution)/shard_map/reduce_scatter | solution.py:59
  540.1 87.1 %copy-start.4 = (bf16[2,256]{1,0:T(2,128)(2,1)S(1)}, bf16[2,256]{1,0:T(2,128)(2,1)}, u32[]{:S(2)}) copy-start(bf16[2,256]{1,0:T(2,128)(2,1)} %param.8) | copy-start | bytes 3076
  540.1 379.1 %copy-start.2 = (bf16[256,128]{0,1:T(8,128)(2,1)S(1)}, bf16[256,128]{0,1:T(8,128)(2,1)}, u32[]{:S(2)}) copy-start(bf16[256,128]{0,1:T(8,128)(2,1)} %reduce-scatter.5.cloned.1.call-done) | copy-start | bytes 196612
  540.2 257.7 %reduce-scatter.11.cloned.1.call-start = ((), (), s32[]{:S(2)}) async-start(), calls=%async_computation.11 | async-start | bytes 1114112 | tf_op jit(solution)/shard_map/reduce_scatter | solution.py:59
  623.6 295.6 %copy-start.3 = (bf16[256,128]{0,1:T(8,128)(2,1)S(1)}, bf16[256,128]{0,1:T(8,128)(2,1)}, u32[]{:S(2)}) copy-start(bf16[256,128]{0,1:T(8,128)(2,1)} %reduce-scatter.9.cloned.1.call-done) | copy-start | bytes 196612
Sparse Core Ops, SparseCore 0:
  10.0 74.8 all-gather.4
  89.7 69.6 all-gather.6
  162.7 124.4 all-gather.8
  289.7 73.4 all-gather.10
  450.7 85.9 reduce-scatter.4
  539.6 84.0 reduce-scatter.8
  626.4 84.1 reduce-scatter.6
  713.7 84.0 reduce-scatter.10
where the time goes:
time: 944 us; the launch traced here: 928 us
  waiting for transfers between devices  641 us (68%)
  blocking collectives  225 us (24%)
  matrix products  38.9 us (4%)
  between operations  14.3 us (2%)
    reduce_scatter x2, waiting for transfers between devices, per_device(): lax.psum_scatter(jnp.dot(weight, head_grad_low, preferred_element_type=jn...  171 us
    reduce_scatter x2, waiting for transfers between devices, per_device(): lax.psum_scatter(lax.dot_general(table, upstream, (((1,), (1,)), ((), ())...  161 us
    all_gather x2, waiting for transfers between devices, per_device(): head_full = lax.all_gather(head_cols, 'vocab', axis=1, tiled=True)  136 us
    all_gather x1, waiting for transfers between devices, per_device(): table = lax.all_gather(unembed, 'seq', axis=0, tiled=True)  128 us
    psum x2, blocking collectives, per_device(): lax.psum((jnp.sum(jnp.exp(logits - top[:, None]), axis=-1), target_part),...  78.6 us
    psum x1, blocking collectives, per_device(): loss_sum, gain_sum = lax.psum((loss_part, gain_part), 'seq')  78.1 us
    all_gather x1, waiting for transfers between devices, per_device(): lax.all_gather(hidden, 'vocab', axis=1, tiled=True)  43.5 us
    pmax x1, blocking collectives, per_device(): top = lax.pmax(local_max, 'vocab')  34.5 us
  transfers between devices with their start and end apart: 8, of which 8 were waited for; matrix products, arithmetic and copies ran while one was open for 3% of the time, Pallas kernels for 0%

commit v1 on v0

v1 whole, which is shorter than its diff:
```python
import jax
import jax.numpy as jnp
from jax import lax
from jax.experimental import pallas as pl
from jax.experimental.pallas import tpu as pltpu
from jax.sharding import PartitionSpec as P

eps = 1e-05
NX, NY, NZ, NFAR, NCORE = 4, 4, 8, 2, 2
NV = NX * NY
PER_Z = NFAR * NCORE
MESH = pl.DeviceIdType.MESH
F32, BF16 = jnp.float32, jnp.bfloat16


def kernel(
    hidden, w_hbm, gains, unembed, targets, weights,
    grad_out, gain_out, loss_out,
    w, xg, hf, table, acc, up, low, tcol, rcol, lossrow,
    stat_x, stat_y, dot_x, dot_y, gain_p, gain_z,
    rs_send, rs_mid, rs_right, rs_left, rs_own, ys_send, ys_recv, head_grad, norm_grad,
    w_sem, xg_sem, hf_sem, far_sem, ring_sem, share_sem, stat_sem, dot_sem, gain_sem, rs_sem,
):
    rows, cols = hidden.shape
    heads = gains.shape[0]
    voc_dev = unembed.shape[1]
    width = cols * NV
    seq, voc = lax.axis_index("seq"), lax.axis_index("vocab")
    x, y = lax.rem(voc, NX), lax.div(voc, NX)
    z, far, core = lax.div(seq, PER_Z), lax.rem(lax.div(seq, NCORE), NFAR), lax.rem(seq, NCORE)
    right, left, over = lax.rem(x + 1, NX), lax.rem(x + 3, NX), lax.rem(x + 2, NX)

    def at_x(j):
        return (seq, y * NX + lax.rem(x + j, NX))

    def at_y(j):
        return (seq, lax.rem(y + j, NY) * NX + x)

    def at_z(j):
        return (lax.rem(z + j, NZ) * PER_Z + far * NCORE + core, voc)

    def at_pair(k):
        other_far = 1 - far if k // 2 else far
        other_core = 1 - core if k % 2 else core
        return (z * PER_Z + other_far * NCORE + other_core, voc)

    pending = []

    def send(src, dst, sems, k, to):
        copy = pltpu.make_async_remote_copy(
            src_ref=src, dst_ref=dst, send_sem=sems.at[0, k], recv_sem=sems.at[1, k],
            device_id=to, device_id_type=MESH,
        )
        copy.start()
        pending.append(copy)

    def arrive(dst, sems, k):
        pltpu.make_async_remote_copy(
            src_ref=dst, dst_ref=dst, send_sem=sems.at[0, k], recv_sem=sems.at[1, k],
            device_id=at_x(1), device_id_type=MESH,
        ).wait_recv()

    w_copy = pltpu.make_async_copy(w_hbm, w, w_sem)
    w_copy.start()
    barrier = pltpu.get_barrier_semaphore()
    partners = (
        [at_x(j) for j in range(1, NX)] + [at_y(j) for j in range(1, NY)]
        + [at_z(j) for j in range(1, NZ)] + [at_pair(k) for k in range(1, 4)]
    )
    for partner in partners:
        pl.semaphore_signal(barrier, inc=1, device_id=partner, device_id_type=MESH)
    xg[voc, 0:rows, :] = hidden[...]
    gain_rows = gains[...].astype(F32)
    gain_pad = jnp.concatenate(
        [jnp.broadcast_to(gain_rows[h : h + 1], (8, cols)) for h in range(heads)], axis=0
    )
    xg[voc, rows : rows + 8 * heads, :] = gain_pad.astype(BF16)
    table[pl.ds(pl.multiple_of(seq * rows, rows), rows), :] = unembed[...]
    pl.semaphore_wait(barrier, len(partners))

    def row(q):
        return lax.rem(y + NY - q, NY) * NX

    def gather_begin(buf, sems):
        for j in range(1, NY):
            send(buf.at[voc], buf.at[voc], sems, j - 1, at_y(j))
        send(buf.at[voc], buf.at[voc], sems, 3, at_x(1))
        send(buf.at[voc], buf.at[voc], sems, 7, at_x(NX - 1))

    def gather_row(buf, sems, q):
        slot = row(q) + x
        arrive(buf.at[slot], sems, q - 1)
        send(buf.at[slot], buf.at[slot], sems, 3 + q, at_x(1))
        send(buf.at[slot], buf.at[slot], sems, 7 + q, at_x(NX - 1))

    def gather_cross(buf, sems, q):
        if q < 2:
            slot, k, to = row(q) + left, 3 + q, at_x(1)
        else:
            slot, k, to = row(q) + right, 7 + q, at_x(NX - 1)
        arrive(buf.at[slot], sems, k)
        send(buf.at[slot], buf.at[slot], sems, 11 + q, to)

    def gather_end(buf, sems):
        for q in (2, 3):
            arrive(buf.at[row(q) + left], sems, 3 + q)
        for q in (0, 1):
            arrive(buf.at[row(q) + right], sems, 7 + q)
        for q in range(NY):
            arrive(buf.at[row(q) + over], sems, 11 + q)

    def slab(zz, e, own=True, first=0, count=rows):
        far_e = 1 - far if e else far
        core_e = core if own else 1 - core
        start = pl.multiple_of((zz * PER_Z + far_e * NCORE + core_e) * rows + first, count)
        return table.at[pl.ds(start, count), :]

    def z_at(j):
        return lax.rem(z + j + NZ, NZ)

    def share(e, k, zz):
        send(slab(zz, e), slab(zz, e), share_sem, e * NZ + k, at_pair(1))

    def ring_begin(e):
        if e:
            arrive(slab(z, 1), far_sem, 0)
        send(slab(z, e), slab(z, e), ring_sem, e * 8, at_z(1))
        send(slab(z, e), slab(z, e), ring_sem, e * 8 + 4, at_z(NZ - 1))
        share(e, 0, z)

    half = rows // 2

    def ring_step(e, h):
        for way, to in ((0, at_z(1)), (1, at_z(NZ - 1))):
            zz = z_at(h if way else -h)
            k = e * 8 + way * 4 + h
            arrive(slab(zz, e), ring_sem, k - 1)
            part = slab(zz, e) if h < 3 else slab(zz, e, True, way * half, half)
            send(part, part, ring_sem, k, to)
            share(e, 2 * h - 1 + way, zz)

    def ring_end(e):
        zz = z_at(4)
        for way in range(2):
            arrive(slab(zz, e, True, way * half, half), ring_sem, e * 8 + way * 4 + 3)
        share(e, 7, zz)

    def consume(e, first, last):
        far_e = 1 - far if e else far

        def body(k, carry):
            dist = lax.div(k + 1, 2)
            zz = lax.rem(z + NZ + dist * (1 - 2 * lax.rem(k, 2)), NZ)
            arrive(slab(zz, e, False), share_sem, e * NZ + k)
            block = zz * NFAR + far_e
            begin = pl.multiple_of(block * cols, cols)
            acc[...] += jnp.dot(hf[block], table[pl.ds(begin, cols), :], preferred_element_type=F32)
            return carry

        lax.fori_loop(first, last, body, 0)

    ring_begin(0)
    gather_begin(xg, xg_sem)
    send(slab(z, 0), slab(z, 0), far_sem, 0, at_pair(2))

    acc[...] = jnp.zeros_like(acc)
    for h in range(heads):
        t_row = targets[h : h + 1, :].astype(F32)
        tcol[h * rows : (h + 1) * rows, :] = jnp.broadcast_to(t_row, (rows, rows)).T
    own_x = hidden[...].astype(F32)

    for q in range(1, NY):
        gather_row(xg, xg_sem, q)
    ring_step(0, 1)
    for q in range(NY):
        gather_cross(xg, xg_sem, q)
    gather_end(xg, xg_sem)
    ring_step(0, 2)

    def square(k, total):
        block = xg[k, 0:rows, :].astype(F32)
        return total + block * block

    squares = lax.fori_loop(0, NV, square, jnp.zeros((rows, cols), F32))
    r = lax.rsqrt(jnp.sum(squares, axis=-1, keepdims=True) / width + eps)
    rcol[...] = jnp.broadcast_to(r, rcol.shape)
    w_copy.wait()

    def project(k, totals):
        scaled = xg[k, 0:rows, :].astype(F32) * rcol[:, 0:1]
        gain_k = xg[k, rows : rows + 8 * heads, :].astype(F32)
        begin = pl.multiple_of(k * cols, cols)
        out = []
        for h in range(heads):
            normed = (scaled * gain_k[8 * h : 8 * h + 1]).astype(BF16)
            out.append(
                totals[h]
                + jnp.dot(normed, w[h, pl.ds(begin, cols), :], preferred_element_type=F32)
            )
        return tuple(out)

    empty = jnp.zeros((rows, cols), F32)
    branches = lax.fori_loop(0, NV, project, (empty,) * heads)
    for h in range(heads):
        hf[voc, h * rows : (h + 1) * rows, :] = (own_x + branches[h]).astype(BF16)
    gather_begin(hf, hf_sem)
    ring_step(0, 3)
    ring_begin(1)
    for q in range(1, NY):
        gather_row(hf, hf_sem, q)
    ring_end(0)
    ring_step(1, 1)
    for q in range(NY):
        gather_cross(hf, hf_sem, q)
    ring_step(1, 2)
    gather_end(hf, hf_sem)

    consume(0, 0, NZ)
    ring_step(1, 3)
    consume(1, 0, 7)
    ring_end(1)
    consume(1, 7, NZ)

    col_ids = lax.broadcasted_iota(jnp.int32, (rows, voc_dev), 1) + voc * voc_dev
    lanes = lax.broadcasted_iota(jnp.int32, (rows, rows), 1)

    def picked(h):
        ids = tcol[h * rows : (h + 1) * rows, 0:1].astype(jnp.int32)
        return col_ids == ids

    def stat_rows(top, total, target):
        line = lax.broadcasted_iota(jnp.int32, (8, top.shape[1]), 0)
        return jnp.where(line == 0, top, jnp.where(line == 1, total, jnp.where(line == 2, target, 0.0)))

    def merge(slots, count):
        tops = [slots[j, 0:1, :] for j in range(count)]
        top = tops[0]
        for other in tops[1:]:
            top = jnp.maximum(top, other)
        total = jnp.zeros_like(top)
        target = jnp.zeros_like(top)
        for j in range(count):
            total = total + slots[j, 1:2, :] * jnp.exp(tops[j] - top)
            target = target + slots[j, 2:3, :]
        return top, total, target

    for h in range(heads):
        logits = acc[h * rows : (h + 1) * rows, :]
        top = jnp.max(logits, axis=-1, keepdims=True)
        total = jnp.sum(jnp.exp(logits - top), axis=-1, keepdims=True)
        target = jnp.sum(jnp.where(picked(h), logits, 0.0), axis=-1, keepdims=True)
        packed = jnp.where(lanes == 0, top, jnp.where(lanes == 1, total, jnp.where(lanes == 2, target, 0.0)))
        stat_x[0, :, h * rows : (h + 1) * rows] = packed.T[0:8, :]
    for j in range(1, NX):
        send(stat_x.at[0], stat_x.at[j], stat_sem, j - 1, at_x(j))
    for j in range(1, NX):
        arrive(stat_x.at[j], stat_sem, j - 1)
    stat_y[0] = stat_rows(*merge(stat_x, NX))
    for j in range(1, NY):
        send(stat_y.at[0], stat_y.at[j], stat_sem, 2 + j, at_y(j))
    for j in range(1, NY):
        arrive(stat_y.at[j], stat_sem, 2 + j)
    top, total, target = merge(stat_y, NY)
    lse = top + jnp.log(total)
    lossrow[...] = jnp.broadcast_to(lse - target, lossrow.shape)
    for h in range(heads):
        lse_col = jnp.broadcast_to(lse[:, h * rows : (h + 1) * rows], (rows, rows)).T[:, 0:1]
        probs = jnp.exp(acc[h * rows : (h + 1) * rows, :] - lse_col)
        upstream = weights[h] * (probs - jnp.where(picked(h), 1.0, 0.0))
        up[h] = upstream.T.astype(BF16)

    def partial(p, h, step, yb):
        block = yb * NX + lax.rem(x + step, NX)
        begin = pl.multiple_of(block * cols, cols)
        if p == 0:
            return jnp.dot(table[pl.ds(begin, cols), :], up[h], preferred_element_type=F32)
        return jnp.dot(w[h, pl.ds(begin, cols), :], low[h], preferred_element_type=F32)

    def reduce_across(p, h):
        i = p * heads + h

        def body(n, carry):
            rs_send[i, n] = partial(p, h, 2, n).astype(BF16)
            return carry

        lax.fori_loop(0, 4, body, 0)
        two, four = pl.ds(0, 2), pl.ds(2, 2)
        send(rs_send.at[i, two], rs_mid.at[i, two], rs_sem.at[i], 0, at_x(1))
        send(rs_send.at[i, four], rs_mid.at[i, four], rs_sem.at[i], 1, at_x(NX - 1))

    def reduce_near(p, h):
        i = p * heads + h

        def body(n, carry):
            g, b = lax.div(n, 2), lax.rem(n, 2)
            rs_send[i, 4 + n] = partial(p, h, 1 + 2 * g, 2 - 2 * g + b).astype(BF16)
            return carry

        lax.fori_loop(0, 4, body, 0)
        send(rs_send.at[i, pl.ds(4, 2)], rs_right.at[i, pl.ds(2, 2)], rs_sem.at[i], 2, at_x(1))
        send(rs_send.at[i, pl.ds(6, 2)], rs_left.at[i, pl.ds(0, 2)], rs_sem.at[i], 3, at_x(NX - 1))

    def reduce_own(p, h):
        i = p * heads + h

        def body(n, carry):
            rs_own[i, n] = partial(p, h, 0, n)
            return carry

        lax.fori_loop(0, 4, body, 0)

    def reduce_pass(p, h):
        i = p * heads + h
        arrive(rs_mid.at[i, pl.ds(0, 2)], rs_sem.at[i], 0)
        arrive(rs_mid.at[i, pl.ds(2, 2)], rs_sem.at[i], 1)

        def body(n, carry):
            g, b = lax.div(n, 2), lax.rem(n, 2)
            so_far = rs_mid[i, n].astype(F32)
            rs_send[i, 8 + n] = (partial(p, h, 1 + 2 * g, 2 * g + b) + so_far).astype(BF16)
            return carry

        lax.fori_loop(0, 4, body, 0)
        send(rs_send.at[i, pl.ds(8, 2)], rs_right.at[i, pl.ds(0, 2)], rs_sem.at[i], 4, at_x(1))
        send(rs_send.at[i, pl.ds(10, 2)], rs_left.at[i, pl.ds(2, 2)], rs_sem.at[i], 5, at_x(NX - 1))

    def reduce_column(p, h):
        i = p * heads + h
        arrive(rs_right.at[i, pl.ds(2, 2)], rs_sem.at[i], 2)
        arrive(rs_left.at[i, pl.ds(0, 2)], rs_sem.at[i], 3)
        arrive(rs_right.at[i, pl.ds(0, 2)], rs_sem.at[i], 4)
        arrive(rs_left.at[i, pl.ds(2, 2)], rs_sem.at[i], 5)
        for j in range(1, NY):
            yb = lax.rem(y + j, NY)
            total = rs_own[i, yb] + rs_right[i, yb].astype(F32) + rs_left[i, yb].astype(F32)
            ys_send[i, j - 1] = total.astype(BF16)
            send(ys_send.at[i, j - 1], ys_recv.at[i, j - 1], rs_sem.at[i], 5 + j, at_y(j))

    def reduce_end(p, h):
        i = p * heads + h
        total = rs_own[i, y] + rs_right[i, y].astype(F32) + rs_left[i, y].astype(F32)
        for j in range(1, NY):
            arrive(ys_recv.at[i, j - 1], rs_sem.at[i], 5 + j)
            total = total + ys_recv[i, j - 1].astype(F32)
        return total

    def head_done(h):
        total = reduce_end(0, h)
        low[h] = total.astype(BF16)
        head_grad[h] = total

    def norm_done(h):
        norm_grad[h] = reduce_end(1, h).T

    reduce_across(0, 0)
    reduce_near(0, 0)
    reduce_own(0, 0)
    reduce_pass(0, 0)
    reduce_across(0, 1)
    reduce_near(0, 1)
    reduce_column(0, 0)
    reduce_own(0, 1)
    reduce_pass(0, 1)
    head_done(0)
    reduce_across(1, 0)
    reduce_near(1, 0)
    reduce_own(1, 0)
    reduce_column(0, 1)
    reduce_pass(1, 0)
    head_done(1)
    reduce_across(1, 1)
    reduce_near(1, 1)
    reduce_own(1, 1)
    reduce_column(1, 0)
    reduce_pass(1, 1)
    norm_done(0)
    reduce_column(1, 1)
    norm_done(1)

    own_x = hidden[...].astype(F32)
    gain_rows = gains[...].astype(F32)
    r = rcol[:, 0:1]
    scaled = jnp.zeros((rows, cols), F32)
    for h in range(heads):
        scaled = scaled + gain_rows[h : h + 1] * norm_grad[h]
    dots = jnp.sum(scaled * own_x, axis=-1, keepdims=True)
    dot_x[0] = jnp.broadcast_to(dots, (rows, rows)).T[0:8, :]
    for j in range(1, NX):
        send(dot_x.at[0], dot_x.at[j], dot_sem, j - 1, at_x(j))
    line = lax.broadcasted_iota(jnp.int32, (8, cols), 0)
    packed = jnp.where(line == heads, lossrow[...], 0.0)
    for h in range(heads):
        part = jnp.sum(norm_grad[h] * own_x * r, axis=0, keepdims=True)
        packed = packed + jnp.where(line == h, part, 0.0)
    gain_p[0] = packed
    for k in range(1, 4):
        send(gain_p.at[0], gain_p.at[k], gain_sem, k - 1, at_pair(k))
    for j in range(1, NX):
        arrive(dot_x.at[j], dot_sem, j - 1)
    dot_y[0] = dot_x[0] + dot_x[1] + dot_x[2] + dot_x[3]
    for j in range(1, NY):
        send(dot_y.at[0], dot_y.at[j], dot_sem, 2 + j, at_y(j))
    for k in range(1, 4):
        arrive(gain_p.at[k], gain_sem, k - 1)
    gain_z[0] = gain_p[0] + gain_p[1] + gain_p[2] + gain_p[3]
    for j in range(1, NZ):
        send(gain_z.at[0], gain_z.at[j], gain_sem, 2 + j, at_z(j))
    for j in range(1, NY):
        arrive(dot_y.at[j], dot_sem, 2 + j)
    dots = dot_y[0] + dot_y[1] + dot_y[2] + dot_y[3]
    dot_col = jnp.broadcast_to(dots[0:1, :], (rows, rows)).T[:, 0:1]
    direct = (head_grad[0] + head_grad[1]).T
    grad_out[...] = direct + r * scaled - own_x * (r * r * r * dot_col / width)
    sums = gain_z[0]
    for j in range(1, NZ):
        arrive(gain_z.at[j], gain_sem, 2 + j)
        sums = sums + gain_z[j]
    gain_out[...] = sums[0:heads, :]
    spot = lax.broadcasted_iota(jnp.int32, loss_out.shape, 1)
    losses = jnp.zeros(loss_out.shape, F32)
    tokens = rows * NZ * PER_Z
    for h in range(heads):
        loss = jnp.sum(sums[heads : heads + 1, h * rows : (h + 1) * rows], axis=-1, keepdims=True)
        losses = losses + jnp.where(spot == h, loss / tokens, 0.0)
    loss_out[...] = losses
    for copy in pending:
        copy.wait_send()


def per_device(hidden, head_weight, gains, unembed, targets, loss_weights):
    rows, cols = hidden.shape
    heads = gains.shape[0]
    voc_dev = unembed.shape[1]
    both = heads * rows
    runs = 2 * heads
    vmem = pl.BlockSpec(memory_space=pltpu.VMEM)
    dma = pltpu.SemaphoreType.DMA
    grad, gain, loss = pl.pallas_call(
        kernel,
        out_shape=(
            jax.ShapeDtypeStruct((rows, cols), F32),
            jax.ShapeDtypeStruct((heads, cols), F32),
            jax.ShapeDtypeStruct((8, 128), F32),
        ),
        in_specs=[
            vmem,
            pl.BlockSpec(memory_space=pl.ANY),
            vmem,
            vmem,
            vmem,
            pl.BlockSpec(memory_space=pltpu.SMEM),
        ],
        out_specs=(vmem, vmem, vmem),
        scratch_shapes=[
            pltpu.VMEM(head_weight.shape, BF16),
            pltpu.VMEM((NV, rows + 8 * heads, cols), BF16),
            pltpu.VMEM((NV, both, cols), BF16),
            pltpu.VMEM((NV * cols, voc_dev), BF16),
            pltpu.VMEM((both, voc_dev), F32),
            pltpu.VMEM((heads, voc_dev, rows), BF16),
            pltpu.VMEM((heads, cols, rows), BF16),
            pltpu.VMEM((both, rows), F32),
            pltpu.VMEM((rows, rows), F32),
            pltpu.VMEM((8, both), F32),
            pltpu.VMEM((NX, 8, both), F32),
            pltpu.VMEM((NY, 8, both), F32),
            pltpu.VMEM((NX, 8, rows), F32),
            pltpu.VMEM((NY, 8, rows), F32),
            pltpu.VMEM((4, 8, cols), F32),
            pltpu.VMEM((NZ, 8, cols), F32),
            pltpu.VMEM((runs, 12, cols, rows), BF16),
            pltpu.VMEM((runs, 4, cols, rows), BF16),
            pltpu.VMEM((runs, 4, cols, rows), BF16),
            pltpu.VMEM((runs, 4, cols, rows), BF16),
            pltpu.VMEM((runs, 4, cols, rows), F32),
            pltpu.VMEM((runs, 3, cols, rows), BF16),
            pltpu.VMEM((runs, 3, cols, rows), BF16),
            pltpu.VMEM((heads, cols, rows), F32),
            pltpu.VMEM((heads, rows, cols), F32),
            dma,
            dma((2, 15)),
            dma((2, 15)),
            dma((2, 1)),
            dma((2, 16)),
            dma((2, 16)),
            dma((2, 6)),
            dma((2, 6)),
            dma((2, 10)),
            dma((runs, 2, 9)),
        ],
        compiler_params=pltpu.CompilerParams(
            collective_id=0, has_side_effects=True, vmem_limit_bytes=52 * 1024 * 1024
        ),
    )(hidden, head_weight, gains, unembed, targets, loss_weights)
    return loss[0, :heads], grad, gain


def solution(mesh):
    in_specs = (
        P("seq", "vocab"),
        P(None, None, "vocab"),
        P(None, "vocab"),
        P("seq", "vocab"),
        P(None, "seq"),
        P(),
    )
    out_specs = (P(), P("seq", "vocab"), P(None, "vocab"))
    return jax.shard_map(
        per_device, mesh=mesh, in_specs=in_specs, out_specs=out_specs, check_vma=False
    )
```

time: 944 us -> 150 us (0.16); the launches traced: 928 us -> 150 us
  waiting for transfers between devices: 641 us -> 0 us
  blocking collectives: 225 us -> 0 us
  Pallas kernels: 0 us -> 143 us
  matrix products: 38.9 us -> 0 us
  between operations: 14.3 us -> 0.65 us
    reduce_scatter x4 -> x0, waiting for transfers between devices: 332 us -> none  [the longest x2 171 us: per_device(): lax.psum_scatter(jnp.dot(weight, head_grad_low, preferred_element_type=jn...]
    all_gather x4 -> x0, waiting for transfers between devices: 308 us -> none  [the longest x2 136 us: per_device(): head_full = lax.all_gather(head_cols, 'vocab', axis=1, tiled=True)]
    psum x3 -> x0, blocking collectives: 157 us -> none  [the longest x2 78.6 us: per_device(): lax.psum((jnp.sum(jnp.exp(logits - top[:, None]), axis=-1), target_part),...]
    pallas_call x0 -> x1, Pallas kernels: none -> 143 us  [per_device(): pl.pallas_call(kernel, out_shape=(jax.ShapeDtypeStruct((rows, cols), F32)...]
    dot_general x8 -> x0, matrix products: 38.9 us -> none  [the longest x2 16 us: per_device(): lax.dot_general(table, upstream, (((1,), (1,)), ((), ())), preferred_elem...]
    pmax x1 -> x0, blocking collectives: 34.5 us -> none  [per_device(): top = lax.pmax(local_max, 'vocab')]
    all_gather x1 -> x0, blocking collectives: 33.4 us -> none  [per_device(): lax.all_gather(gains, 'vocab', axis=1, tiled=True)]
  transfers between devices with their start and end apart: 8 -> 0, of which waited for: 8 -> 0; matrix products, arithmetic and copies ran while one was open for 3% -> 0% of each run, Pallas kernels for 0% -> 0%
where the time goes in v1:
time: 150 us
  Pallas kernels  143 us (95%)
  local copies, waits for them, and re-layouts  5.54 us (4%)
    pallas_call x1, Pallas kernels, per_device(): pl.pallas_call(kernel, out_shape=(jax.ShapeDtypeStruct((rows, cols), F32)...  143 us
    unnamed x12, local copies, waits for them, and re-layouts  5.03 us

profile of v1, /device:TPU:56, one launch (start us, length us, event | category | flops | bytes accessed | tf_op | source)
XLA Modules:
  0.0 149.7 jit_solution(6471413404484511434)
XLA Ops:
  0.6 0.0 copy-start
  0.6 0.9 copy-done
  1.6 0.0 copy-start.1
  1.6 0.8 copy-done.1
  2.4 0.0 copy-start.2
  2.4 0.7 copy-done.2
  3.1 0.0 copy-start.3
  3.1 0.7 copy-done.3
  3.8 0.0 copy-start.4
  3.8 0.7 copy-done.4
  4.4 143.5 %shard_map.85 = (f32[128,256]{1,0:T(8,128)S(1)}, f32[2,256]{1,0:T(2,128)S(1)}, f32[8,128]{1,0:T(8,128)S(1)}) custom-call(bf16[128,256]{1,0:T(8,128)(2,1)S(1)} %copy-done.1, bf16[2,4096,256]{2,1,0:T(8,128)(2,1)} %w_hbm.1, bf16[2,256]{1,0:T(2,128)(2,1)S(1)} %copy-done.2, bf16[128,1024]{1,0:T(8,128)(2,1)S(1)} %copy-done, s32[2,128]{1,0:T(2,128)S(1)} %copy-done.3, ...), custom_call_target="tpu_custom_call" | custom-call | tf_op jit(solution)/shard_map/pallas_call | solution.py:438
  147.9 0.5 slice_bitcast_fusion
  148.5 0.7 copy.11
  149.1 0.6 copy.12
Async XLA Ops:
  0.6 1.0 copy-start
  1.6 0.8 copy-start.1
  2.4 0.7 copy-start.2
  3.1 0.7 copy-start.3
  3.8 0.7 copy-start.4

commit v2 on v1

v2 whole, which is shorter than its diff:
```python
import jax
import jax.numpy as jnp
from jax import lax
from jax.experimental import pallas as pl
from jax.experimental.pallas import tpu as pltpu
from jax.sharding import PartitionSpec as P

eps = 1e-05
NX, NY, NZ, NFAR, NCORE = 4, 4, 8, 2, 2
NV = NX * NY
PER_Z = NFAR * NCORE
MESH = pl.DeviceIdType.MESH
F32, BF16 = jnp.float32, jnp.bfloat16


def kernel(
    hidden_hbm, w_hbm, gains_hbm, unembed_hbm, targets_hbm, weights_hbm,
    grad_out, gain_out, loss_out,
    w, gains, targets, weights, xg, hf, normed, table, relay, acc, acc_t, up, low,
    x_t, gain_cols, rcol, r_line, lossrow, gain_rows,
    stat_x, stat_y, dot_x, dot_y, gain_p, gain_z,
    rs_send, rs_in, rs_part, rs_own, ys_send, ys_recv, head_grad, norm_grad,
    local_sem, xg_sem, hf_sem, far_sem, ring_sem, share_sem, stat_sem, dot_sem, gain_sem, rs_sem,
):
    rows, cols = hidden_hbm.shape
    heads = gains.shape[0]
    both = heads * rows
    voc_dev = unembed_hbm.shape[1]
    width = cols * NV
    seq, voc = lax.axis_index("seq"), lax.axis_index("vocab")
    x, y = lax.rem(voc, NX), lax.div(voc, NX)
    z, far, core = lax.div(seq, PER_Z), lax.rem(lax.div(seq, NCORE), NFAR), lax.rem(seq, NCORE)
    right, left, over = lax.rem(x + 1, NX), lax.rem(x + 3, NX), lax.rem(x + 2, NX)
    levels = NFAR * NY
    level = far * NY + y

    def at_x(j):
        return (seq, y * NX + lax.rem(x + j, NX))

    def at_y(j):
        return (seq, lax.rem(y + j, NY) * NX + x)

    def at_z(j):
        return (lax.rem(z + j, NZ) * PER_Z + far * NCORE + core, voc)

    def at_pair(k):
        other_far = 1 - far if k // 2 else far
        other_core = 1 - core if k % 2 else core
        return (z * PER_Z + other_far * NCORE + other_core, voc)

    def at_level(j):
        other = lax.rem(level + j + levels, levels)
        return (z * PER_Z + lax.div(other, NY) * NCORE + core, lax.rem(other, NY) * NX + x)

    pending = []

    def send(src, dst, sems, k, to):
        copy = pltpu.make_async_remote_copy(
            src_ref=src, dst_ref=dst, send_sem=sems.at[0, k], recv_sem=sems.at[1, k],
            device_id=to, device_id_type=MESH,
        )
        copy.start()
        pending.append(copy)

    def arrive(dst, sems, k):
        pltpu.make_async_remote_copy(
            src_ref=dst, dst_ref=dst, send_sem=sems.at[0, k], recv_sem=sems.at[1, k],
            device_id=at_x(1), device_id_type=MESH,
        ).wait_recv()

    own_rows = pl.ds(pl.multiple_of(seq * rows, rows), rows)
    fetches = [
        pltpu.make_async_copy(hidden_hbm, xg.at[voc, pl.ds(0, rows), :], local_sem.at[0]),
        pltpu.make_async_copy(unembed_hbm, table.at[own_rows, :], local_sem.at[1]),
        pltpu.make_async_copy(gains_hbm, gains, local_sem.at[2]),
        pltpu.make_async_copy(targets_hbm, targets, local_sem.at[3]),
        pltpu.make_async_copy(weights_hbm, weights, local_sem.at[4]),
        pltpu.make_async_copy(w_hbm, w, local_sem.at[5]),
    ]
    for fetch in fetches:
        fetch.start()
    barrier = pltpu.get_barrier_semaphore()
    partners = (
        [at_x(j) for j in range(1, NX)] + [at_y(j) for j in range(1, NY)]
        + [at_z(j) for j in range(1, NZ)] + [at_pair(k) for k in range(1, 4)]
        + [at_level(2), at_level(-2)]
    )
    for partner in partners:
        pl.semaphore_signal(barrier, inc=1, device_id=partner, device_id_type=MESH)
    for k in range(5):
        fetches[k].wait()
    gain_lines = gains[...].astype(F32)
    gain_pad = jnp.concatenate(
        [jnp.broadcast_to(gain_lines[h : h + 1], (8, cols)) for h in range(heads)], axis=0
    )
    xg[voc, rows : rows + 8 * heads, :] = gain_pad.astype(BF16)
    pl.semaphore_wait(barrier, len(partners))

    def row(q):
        return lax.rem(y + NY - q, NY) * NX

    def gather_begin(at, sems, base):
        for j in range(1, NY):
            send(at(voc), at(voc), sems, base + j - 1, at_y(j))
        send(at(voc), at(voc), sems, base + 3, at_x(1))
        send(at(voc), at(voc), sems, base + 7, at_x(NX - 1))

    def gather_row(at, sems, base, q):
        slot = row(q) + x
        arrive(at(slot), sems, base + q - 1)
        send(at(slot), at(slot), sems, base + 3 + q, at_x(1))
        send(at(slot), at(slot), sems, base + 7 + q, at_x(NX - 1))

    def gather_cross(at, sems, base, q):
        if q < 2:
            slot, k, to = row(q) + left, 3 + q, at_x(1)
        else:
            slot, k, to = row(q) + right, 7 + q, at_x(NX - 1)
        arrive(at(slot), sems, base + k)
        send(at(slot), at(slot), sems, base + 11 + q, to)

    def gather_end(at, sems, base):
        for q in (2, 3):
            arrive(at(row(q) + left), sems, base + 3 + q)
        for q in (0, 1):
            arrive(at(row(q) + right), sems, base + 7 + q)
        for q in range(NY):
            arrive(at(row(q) + over), sems, base + 11 + q)

    def x_at(slot):
        return xg.at[slot]

    def hf_at(h):
        return lambda slot: hf.at[slot, pl.ds(h * rows, rows), :]

    def slab(zz, e, own=True, first=0, count=rows):
        far_e = 1 - far if e else far
        core_e = core if own else 1 - core
        start = pl.multiple_of((zz * PER_Z + far_e * NCORE + core_e) * rows + first, count)
        return table.at[pl.ds(start, count), :]

    def z_at(j):
        return lax.rem(z + j + NZ, NZ)

    def share(e, k, zz):
        send(slab(zz, e), slab(zz, e), share_sem, e * NZ + k, at_pair(1))

    half = rows // 2

    def part_of(zz, e, p):
        return slab(zz, e, True, p * half, half)

    leg = 2 - 4 * core

    def far_begin():
        for p in range(2):
            send(part_of(z, 0, p), relay.at[p], far_sem, p, at_level(leg))

    def far_pass(p):
        arrive(relay.at[p], far_sem, p)
        source = lax.rem(level - leg + levels, levels)
        begin = (z * PER_Z + lax.div(source, NY) * NCORE + core) * rows + p * half
        place = table.at[pl.ds(pl.multiple_of(begin, half), half), :]
        send(relay.at[p], place, far_sem, 2 + p, at_level(leg))

    def ring_send(zz, e, way, h, p):
        block = part_of(zz, e, p)
        send(block, block, ring_sem, e * 14 + way * 7 + (h - 1) * 2 + (p if h < 4 else 0),
             at_z(NZ - 1 if way else 1))

    def ring_arrive(zz, e, way, h, p):
        arrive(part_of(zz, e, p), ring_sem, e * 14 + way * 7 + (h - 1) * 2 + (p if h < 4 else 0))

    def ring_begin(e, turn):
        if e:
            arrive(part_of(z, 1, turn), far_sem, 2 + turn)
        for way in range(2):
            ring_send(z, e, way, 1, turn if e else way ^ turn)
        if turn:
            share(e, 0, z)

    def ring_step(e, h, turn):
        for way in range(2):
            p = turn if e and h == 1 else way ^ turn
            zz = z_at(h if way else -h)
            ring_arrive(zz, e, way, h, p)
            if h < 3 or p == way:
                ring_send(zz, e, way, h + 1, p)
            if turn:
                share(e, 2 * h - 1 + way, zz)

    def ring_end(e):
        zz = z_at(4)
        for way in range(2):
            ring_arrive(zz, e, way, 4, way)
        share(e, 7, zz)

    def consume(e, first, last):
        far_e = 1 - far if e else far

        def body(k, carry):
            dist = lax.div(k + 1, 2)
            zz = lax.rem(z + NZ + dist * (1 - 2 * lax.rem(k, 2)), NZ)
            arrive(slab(zz, e, False), share_sem, e * NZ + k)
            block = zz * NFAR + far_e
            begin = pl.multiple_of(block * cols, cols)
            acc[...] += jnp.dot(hf[block], table[pl.ds(begin, cols), :], preferred_element_type=F32)
            return carry

        lax.fori_loop(first, last, body, 0)

    gather_begin(x_at, xg_sem, 0)
    ring_begin(0, 0)
    far_begin()
    ring_begin(0, 1)

    acc[...] = jnp.zeros_like(acc)
    own_x = xg[voc, 0:rows, :].astype(F32)
    x_t[...] = own_x.T
    for h in range(heads):
        gain_cols[h] = jnp.broadcast_to(gain_lines[h : h + 1], (rows, cols)).T

    for q in range(1, NY):
        gather_row(x_at, xg_sem, 0, q)
    ring_step(0, 1, 0)
    far_pass(0)
    gather_cross(x_at, xg_sem, 0, 0)
    gather_cross(x_at, xg_sem, 0, 2)
    ring_step(0, 1, 1)
    far_pass(1)
    gather_cross(x_at, xg_sem, 0, 1)
    gather_cross(x_at, xg_sem, 0, 3)
    ring_step(0, 2, 0)
    ring_begin(1, 0)
    ring_step(0, 2, 1)
    gather_end(x_at, xg_sem, 0)

    def square(k, total):
        block = xg[k, 0:rows, :].astype(F32)
        return total + block * block

    squares = lax.fori_loop(0, NV, square, jnp.zeros((rows, cols), F32))
    r = lax.rsqrt(jnp.sum(squares, axis=-1, keepdims=True) / width + eps)
    r_wide = jnp.broadcast_to(r, rcol.shape)
    rcol[...] = r_wide
    r_line[...] = r_wide.T[0:8, :]

    def norm(k, carry):
        scaled = xg[k, 0:rows, :].astype(F32) * rcol[:, 0:1]
        gain_k = xg[k, rows : rows + 8 * heads, :].astype(F32)
        begin = pl.multiple_of(k * cols, cols)
        for h in range(heads):
            normed[h, :, pl.ds(begin, cols)] = (scaled * gain_k[8 * h : 8 * h + 1]).astype(BF16)
        return carry

    ring_begin(1, 1)
    lax.fori_loop(0, NV, norm, 0)
    ring_step(0, 3, 0)
    fetches[5].wait()
    for h in range(heads):
        branch = jnp.dot(normed[h], w[h], preferred_element_type=F32)
        hf[voc, h * rows : (h + 1) * rows, :] = (own_x + branch).astype(BF16)
        gather_begin(hf_at(h), hf_sem, 15 * h)
        if h == 0:
            ring_step(1, 1, 0)
            ring_step(0, 3, 1)
    ring_step(1, 1, 1)
    for q in range(1, NY):
        gather_row(hf_at(0), hf_sem, 0, q)
    ring_end(0)
    ring_step(1, 2, 0)
    for q in range(1, NY):
        gather_row(hf_at(1), hf_sem, 15, q)
    for q in range(NY):
        gather_cross(hf_at(0), hf_sem, 0, q)
    ring_step(1, 2, 1)
    gather_cross(hf_at(1), hf_sem, 15, 0)
    gather_cross(hf_at(1), hf_sem, 15, 2)
    ring_step(1, 3, 0)
    gather_cross(hf_at(1), hf_sem, 15, 1)
    gather_cross(hf_at(1), hf_sem, 15, 3)
    gather_end(hf_at(0), hf_sem, 0)
    gather_end(hf_at(1), hf_sem, 15)

    consume(0, 0, 5)
    ring_step(1, 3, 1)
    consume(0, 5, NZ)
    consume(1, 0, 7)
    ring_end(1)
    consume(1, 7, NZ)

    step = 128
    ids = jnp.concatenate([targets[h : h + 1, :] for h in range(heads)], axis=1) - voc * voc_dev
    chunk_ids = lax.broadcasted_iota(jnp.int32, (step, both), 0)
    lane = lax.broadcasted_iota(jnp.int32, (1, both), 1)
    weight_row = jnp.full((1, both), weights[0], F32)
    for h in range(1, heads):
        weight_row = jnp.where(lane >= h * rows, weights[h], weight_row)

    def stat_rows(top, total, target):
        line = lax.broadcasted_iota(jnp.int32, (8, both), 0)
        return jnp.where(line == 0, top, jnp.where(line == 1, total, jnp.where(line == 2, target, 0.0)))

    def merge(slots, count):
        tops = [slots[j, 0:1, :] for j in range(count)]
        top = tops[0]
        for other in tops[1:]:
            top = jnp.maximum(top, other)
        total = jnp.zeros_like(top)
        target = jnp.zeros_like(top)
        for j in range(count):
            total = total + slots[j, 1:2, :] * jnp.exp(tops[j] - top)
            target = target + slots[j, 2:3, :]
        return top, total, target

    def turn(k, top):
        begin = pl.multiple_of(k * step, step)
        chunk = acc[:, pl.ds(begin, step)].T
        acc_t[pl.ds(begin, step), :] = chunk
        return jnp.maximum(top, jnp.max(chunk, axis=0, keepdims=True))

    first_chunk = acc[:, 0:step].T
    acc_t[0:step, :] = first_chunk
    top = lax.fori_loop(1, voc_dev // step, turn, jnp.max(first_chunk, axis=0, keepdims=True))

    def gauge(k, sums):
        begin = pl.multiple_of(k * step, step)
        chunk = acc_t[pl.ds(begin, step), :]
        total = jnp.sum(jnp.exp(chunk - top), axis=0, keepdims=True)
        hit = jnp.where(chunk_ids == ids - begin, chunk, 0.0)
        return sums[0] + total, sums[1] + jnp.sum(hit, axis=0, keepdims=True)

    empty = jnp.zeros((1, both), F32)
    total, target = lax.fori_loop(0, voc_dev // step, gauge, (empty, empty))
    stat_x[0] = stat_rows(top, total, target)
    for j in range(1, NX):
        send(stat_x.at[0], stat_x.at[j], stat_sem, j - 1, at_x(j))
    for j in range(1, NX):
        arrive(stat_x.at[j], stat_sem, j - 1)
    stat_y[0] = stat_rows(*merge(stat_x, NX))
    for j in range(1, NY):
        send(stat_y.at[0], stat_y.at[j], stat_sem, 2 + j, at_y(j))
    for j in range(1, NY):
        arrive(stat_y.at[j], stat_sem, 2 + j)
    top, total, target = merge(stat_y, NY)
    lse = top + jnp.log(total)
    lossrow[...] = jnp.broadcast_to(lse - target, lossrow.shape)

    def pull(k, carry):
        begin = pl.multiple_of(k * step, step)
        probs = jnp.exp(acc_t[pl.ds(begin, step), :] - lse)
        hit = jnp.where(chunk_ids == ids - begin, 1.0, 0.0)
        up[pl.ds(begin, step), :] = (weight_row * (probs - hit)).astype(BF16)
        return carry

    lax.fori_loop(0, voc_dev // step, pull, 0)

    def block_rows(way, yb):
        block = yb * NX + lax.rem(x + way, NX)
        return pl.ds(pl.multiple_of(block * cols, cols), cols)

    def head_part(way, yb):
        out = jnp.dot(table[block_rows(way, yb), :], up[...], preferred_element_type=F32)
        return [out[:, h * rows : (h + 1) * rows] for h in range(heads)]

    def norm_part(h, way, yb):
        return jnp.dot(w[h, block_rows(way, yb), :], low[h], preferred_element_type=F32)

    def across_of(n):
        way, b = lax.rem(n, 2), lax.div(n, 2)
        return way, 2 * way + b, 2 * way + b

    def near_of(n):
        way, b = lax.rem(n, 2), lax.div(n, 2)
        yb = 2 - 2 * way + b
        return way, yb, 4 + 4 * way + yb

    def last_of(n):
        way, b = lax.rem(n, 2), lax.div(n, 2)
        yb = 2 * way + b
        return way, yb, 4 + 4 * way + yb

    def loop4(body):
        def run(n, carry):
            body(n)
            return carry

        lax.fori_loop(0, 4, run, 0)

    def x_copy(i, way, slot):
        return pltpu.make_async_remote_copy(
            src_ref=rs_send.at[i, slot], dst_ref=rs_in.at[i, slot],
            send_sem=rs_sem.at[i, 0, slot], recv_sem=rs_sem.at[i, 1, slot],
            device_id=at_x(1 + 2 * way), device_id_type=MESH,
        )

    def x_arrive(i, slot):
        x_copy(i, 0, slot).wait_recv()

    def y_copy(i, yb):
        return pltpu.make_async_remote_copy(
            src_ref=ys_send.at[i, yb], dst_ref=ys_recv.at[i, y],
            send_sem=rs_sem.at[i, 0, 12 + yb], recv_sem=rs_sem.at[i, 1, 12 + y],
            device_id=(seq, yb * NX + x), device_id_type=MESH,
        )

    def y_arrive(i, yb):
        pltpu.make_async_remote_copy(
            src_ref=ys_send.at[i, yb], dst_ref=ys_recv.at[i, yb],
            send_sem=rs_sem.at[i, 0, 12 + yb], recv_sem=rs_sem.at[i, 1, 12 + yb],
            device_id=(seq, yb * NX + x), device_id_type=MESH,
        ).wait_recv()

    def column(i):
        for k in range(2):
            for yb in (k, k + 2):
                x_arrive(i, 4 + yb)
                x_arrive(i, 8 + yb)
                total = rs_own[i, yb] + rs_in[i, 4 + yb].astype(F32) + rs_in[i, 8 + yb].astype(F32)
                rs_own[i, yb] = total
                ys_send[i, yb] = total.astype(BF16)

                @pl.when(y != yb)
                def _():
                    y_copy(i, yb).start()

    def finish(i):
        total = rs_own[i, y]
        for j in range(1, NY):
            peer = lax.rem(y + j, NY)
            y_arrive(i, peer)
            total = total + ys_recv[i, peer].astype(F32)
        return total

    def across_heads(n):
        way, yb, slot = across_of(n)
        for h, part in enumerate(head_part(2, yb)):
            rs_send[h, slot] = part.astype(BF16)
        x_copy(0, way, slot).start()

    def near_heads(n):
        way, yb, slot = near_of(n)
        for h, part in enumerate(head_part(1 + 2 * way, yb)):
            rs_send[h, slot] = part.astype(BF16)
        x_copy(0, way, slot).start()

    def last_heads(n):
        way, yb, slot = last_of(n)
        for h, part in enumerate(head_part(1 + 2 * way, yb)):
            rs_part[h, yb] = part

    def own_heads(n):
        for h, part in enumerate(head_part(0, n)):
            rs_own[h, n] = part

    def send_heads(h):
        def across(n):
            way, yb, slot = across_of(n)
            x_copy(h, way, slot).start()

        def near(n):
            way, yb, slot = near_of(n)
            x_copy(h, way, slot).start()

        loop4(across)
        loop4(near)

    def pass_heads(h):
        def body(n):
            way, yb, slot = last_of(n)
            x_arrive(h, yb)
            rs_send[h, slot] = (rs_part[h, yb] + rs_in[h, yb].astype(F32)).astype(BF16)
            x_copy(h, way, slot).start()

        loop4(body)

    def head_done(h):
        total = finish(h)
        low[h] = total.astype(BF16)
        head_grad[h] = total

    def norm_begin(h):
        i = heads + h

        def across(n):
            way, yb, slot = across_of(n)
            rs_send[i, slot] = norm_part(h, 2, yb).astype(BF16)
            x_copy(i, way, slot).start()

        def near(n):
            way, yb, slot = near_of(n)
            rs_send[i, slot] = norm_part(h, 1 + 2 * way, yb).astype(BF16)
            x_copy(i, way, slot).start()

        loop4(across)
        loop4(near)

    def norm_pass(h):
        i = heads + h

        def own(n):
            rs_own[i, n] = norm_part(h, 0, n)

        def last(n):
            way, yb, slot = last_of(n)
            part = norm_part(h, 1 + 2 * way, yb)
            x_arrive(i, yb)
            rs_send[i, slot] = (part + rs_in[i, yb].astype(F32)).astype(BF16)
            x_copy(i, way, slot).start()

        loop4(own)
        loop4(last)

    def norm_done(h):
        norm_grad[h] = finish(heads + h)

    def gain_done(h):
        weighed = norm_grad[h] * x_t[...] * r_line[0:1, :]
        part = jnp.sum(weighed.T, axis=0, keepdims=True)
        gain_rows[8 * h : 8 * h + 8, :] = jnp.broadcast_to(part, (8, cols))

    loop4(across_heads)
    loop4(near_heads)
    loop4(last_heads)
    pass_heads(0)
    send_heads(1)
    loop4(own_heads)
    column(0)
    pass_heads(1)
    head_done(0)
    norm_begin(0)
    column(1)
    norm_pass(0)
    head_done(1)
    norm_begin(1)
    column(2)
    norm_pass(1)
    norm_done(0)
    gain_done(0)
    column(3)
    norm_done(1)

    scaled = jnp.zeros((cols, rows), F32)
    for h in range(heads):
        scaled = scaled + gain_cols[h] * norm_grad[h]
    dots = jnp.sum(scaled * x_t[...], axis=0, keepdims=True)
    dot_x[0] = jnp.broadcast_to(dots, (8, rows))
    for j in range(1, NX):
        send(dot_x.at[0], dot_x.at[j], dot_sem, j - 1, at_x(j))
    for h in range(1, heads):
        gain_done(h)
    line = lax.broadcasted_iota(jnp.int32, (8, cols), 0)
    packed = jnp.where(line == heads, lossrow[...], 0.0)
    for h in range(heads):
        packed = packed + jnp.where(line == h, gain_rows[8 * h : 8 * h + 8, :], 0.0)
    gain_p[0] = packed
    for k in range(1, 4):
        send(gain_p.at[0], gain_p.at[k], gain_sem, k - 1, at_pair(k))
    for j in range(1, NX):
        arrive(dot_x.at[j], dot_sem, j - 1)
    dot_y[0] = dot_x[0] + dot_x[1] + dot_x[2] + dot_x[3]
    for j in range(1, NY):
        send(dot_y.at[0], dot_y.at[j], dot_sem, 2 + j, at_y(j))
    r_row = r_line[0:1, :]
    direct = (head_grad[0] + head_grad[1] + r_row * scaled).T
    for k in range(1, 4):
        arrive(gain_p.at[k], gain_sem, k - 1)
    gain_z[0] = gain_p[0] + gain_p[1] + gain_p[2] + gain_p[3]
    for j in range(1, NZ):
        send(gain_z.at[0], gain_z.at[j], gain_sem, 2 + j, at_z(j))
    for j in range(1, NY):
        arrive(dot_y.at[j], dot_sem, 2 + j)
    dots = dot_y[0] + dot_y[1] + dot_y[2] + dot_y[3]
    back = r_row * r_row * r_row * dots[0:1, :] / width
    back_col = jnp.broadcast_to(back, (rows, rows)).T[:, 0:1]
    grad_out[...] = direct - xg[voc, 0:rows, :].astype(F32) * back_col
    sums = gain_z[0]
    for j in range(1, NZ):
        arrive(gain_z.at[j], gain_sem, 2 + j)
        sums = sums + gain_z[j]
    gain_out[...] = sums[0:heads, :]
    spot = lax.broadcasted_iota(jnp.int32, loss_out.shape, 1)
    losses = jnp.zeros(loss_out.shape, F32)
    tokens = rows * NZ * PER_Z
    for h in range(heads):
        loss = jnp.sum(sums[heads : heads + 1, h * rows : (h + 1) * rows], axis=-1, keepdims=True)
        losses = losses + jnp.where(spot == h, loss / tokens, 0.0)
    loss_out[...] = losses
    for copy in pending:
        copy.wait_send()
    for i in range(2 * heads):
        for slot in range(12):
            x_copy(i, 0, slot).wait_send()
        for j in range(1, NY):
            y_copy(i, lax.rem(y + j, NY)).wait_send()


def per_device(hidden, head_weight, gains, unembed, targets, loss_weights):
    rows, cols = hidden.shape
    heads = gains.shape[0]
    voc_dev = unembed.shape[1]
    both = heads * rows
    runs = 2 * heads
    vmem = pl.BlockSpec(memory_space=pltpu.VMEM)
    dma = pltpu.SemaphoreType.DMA
    grad, gain, loss = pl.pallas_call(
        kernel,
        out_shape=(
            jax.ShapeDtypeStruct((rows, cols), F32),
            jax.ShapeDtypeStruct((heads, cols), F32),
            jax.ShapeDtypeStruct((8, 128), F32),
        ),
        in_specs=[pl.BlockSpec(memory_space=pltpu.HBM)] * 6,
        out_specs=(vmem, vmem, vmem),
        scratch_shapes=[
            pltpu.VMEM(head_weight.shape, BF16),
            pltpu.VMEM(gains.shape, BF16),
            pltpu.VMEM(targets.shape, jnp.int32),
            pltpu.SMEM(loss_weights.shape, F32),
            pltpu.VMEM((NV, rows + 8 * heads, cols), BF16),
            pltpu.VMEM((NV, both, cols), BF16),
            pltpu.VMEM((heads, rows, NV * cols), BF16),
            pltpu.VMEM((NV * cols, voc_dev), BF16),
            pltpu.VMEM((2, rows // 2, voc_dev), BF16),
            pltpu.VMEM((both, voc_dev), F32),
            pltpu.VMEM((voc_dev, both), F32),
            pltpu.VMEM((voc_dev, both), BF16),
            pltpu.VMEM((heads, cols, rows), BF16),
            pltpu.VMEM((cols, rows), F32),
            pltpu.VMEM((heads, cols, rows), F32),
            pltpu.VMEM((rows, rows), F32),
            pltpu.VMEM((8, rows), F32),
            pltpu.VMEM((8, both), F32),
            pltpu.VMEM((8 * heads, cols), F32),
            pltpu.VMEM((NX, 8, both), F32),
            pltpu.VMEM((NY, 8, both), F32),
            pltpu.VMEM((NX, 8, rows), F32),
            pltpu.VMEM((NY, 8, rows), F32),
            pltpu.VMEM((4, 8, cols), F32),
            pltpu.VMEM((NZ, 8, cols), F32),
            pltpu.VMEM((runs, 12, cols, rows), BF16),
            pltpu.VMEM((runs, 12, cols, rows), BF16),
            pltpu.VMEM((heads, 4, cols, rows), F32),
            pltpu.VMEM((runs, 4, cols, rows), F32),
            pltpu.VMEM((runs, 4, cols, rows), BF16),
            pltpu.VMEM((runs, 4, cols, rows), BF16),
            pltpu.VMEM((heads, cols, rows), F32),
            pltpu.VMEM((heads, cols, rows), F32),
            dma((6,)),
            dma((2, 15)),
            dma((2, 15 * heads)),
            dma((2, 4)),
            dma((2, 28)),
            dma((2, 16)),
            dma((2, 6)),
            dma((2, 6)),
            dma((2, 10)),
            dma((runs, 2, 16)),
        ],
        compiler_params=pltpu.CompilerParams(
            collective_id=0, has_side_effects=True, vmem_limit_bytes=60 * 1024 * 1024
        ),
    )(hidden, head_weight, gains, unembed, targets, loss_weights)
    return loss[0, :heads], grad, gain


def solution(mesh):
    in_specs = (
        P("seq", "vocab"),
        P(None, None, "vocab"),
        P(None, "vocab"),
        P("seq", "vocab"),
        P(None, "seq"),
        P(),
    )
    out_specs = (P(), P("seq", "vocab"), P(None, "vocab"))
    return jax.shard_map(
        per_device, mesh=mesh, in_specs=in_specs, out_specs=out_specs, check_vma=False
    )
```

time: 150 us -> 136 us (0.907)
  Pallas kernels: 143 us -> 131 us
  local copies, waits for them, and re-layouts: 5.54 us -> 3.99 us
    pallas_call x1, Pallas kernels: 143 us -> 131 us  [per_device(): pl.pallas_call(kernel, out_shape=(jax.ShapeDtypeStruct((rows, cols), F32)...]
    unnamed x12 -> x2, local copies, waits for them, and re-layouts: 5.03 us -> 2.8 us
where the time goes in v2:
time: 136 us
  Pallas kernels  131 us (96%)
  local copies, waits for them, and re-layouts  3.99 us (3%)
    pallas_call x1, Pallas kernels, per_device(): pl.pallas_call(kernel, out_shape=(jax.ShapeDtypeStruct((rows, cols), F32)...  131 us
    unnamed x2, local copies, waits for them, and re-layouts  2.8 us

profile of v2, /device:TPU:56, one launch (start us, length us, event | category | flops | bytes accessed | tf_op | source)
XLA Modules:
  0.0 135.6 jit_solution(120010714975183020)
XLA Ops:
  0.6 130.9 %shard_map.85 = (f32[128,256]{1,0:T(8,128)}, f32[2,256]{1,0:T(2,128)}, f32[8,128]{1,0:T(8,128)}) custom-call(bf16[128,256]{1,0:T(8,128)(2,1)} %hidden_hbm.1, bf16[2,4096,256]{2,1,0:T(8,128)(2,1)} %w_hbm.1, bf16[2,256]{1,0:T(2,128)(2,1)} %gains_hbm.1, bf16[128,1024]{1,0:T(8,128)(2,1)} %unembed_hbm.1, s32[2,128]{1,0:T(2,128)} %targets_hbm.1, f32[2]{0:T(128)} %weights_hbm.1), custom_call_target="tpu_custom_call" | custom-call | tf_op jit(solution)/shard_map/pallas_call | solution.py:606
  131.6 1.2 slice_bitcast_fusion
  132.8 1.6 %copy.11 = f32[128,256]{1,0:T(8,128)} copy(f32[128,256]{1,0:T(8,128)} %get-tuple-element.13) | data formatting | bytes 262144
  134.3 1.2 copy.12

commit v3 on v2

--- a/solution.py
+++ b/solution.py
@@ -127,11 +127,14 @@
         for q in range(NY):
             arrive(at(row(q) + over), sems, base + 11 + q)
 
-    def x_at(slot):
-        return xg.at[slot]
-
-    def hf_at(h):
-        return lambda slot: hf.at[slot, pl.ds(h * rows, rows), :]
+    half = rows // 2
+    pads = 8 * heads
+
+    def x_at(t):
+        return lambda slot: xg.at[slot, pl.ds(t * half, half + t * pads), :]
+
+    def hf_at(t):
+        return lambda slot: hf.at[slot, pl.ds(t * rows, rows), :]
 
     def slab(zz, e, own=True, first=0, count=rows):
         far_e = 1 - far if e else far
@@ -144,8 +147,6 @@
 
     def share(e, k, zz):
         send(slab(zz, e), slab(zz, e), share_sem, e * NZ + k, at_pair(1))
-
-    half = rows // 2
 
     def part_of(zz, e, p):
         return slab(zz, e, True, p * half, half)
@@ -204,14 +205,21 @@
             arrive(slab(zz, e, False), share_sem, e * NZ + k)
             block = zz * NFAR + far_e
             begin = pl.multiple_of(block * cols, cols)
-            acc[...] += jnp.dot(hf[block], table[pl.ds(begin, cols), :], preferred_element_type=F32)
+            lines = [
+                hf[block, t * rows + h * half : t * rows + (h + 1) * half, :]
+                for h in range(heads) for t in range(2)
+            ]
+            acc[...] += jnp.dot(
+                jnp.concatenate(lines, axis=0), table[pl.ds(begin, cols), :],
+                preferred_element_type=F32,
+            )
             return carry
 
         lax.fori_loop(first, last, body, 0)
 
-    gather_begin(x_at, xg_sem, 0)
+    for t in (1, 0):
+        gather_begin(x_at(t), xg_sem, 15 * t)
     ring_begin(0, 0)
-    far_begin()
     ring_begin(0, 1)
 
     acc[...] = jnp.zeros_like(acc)
@@ -220,72 +228,82 @@
     for h in range(heads):
         gain_cols[h] = jnp.broadcast_to(gain_lines[h : h + 1], (rows, cols)).T
 
+    def project(t):
+        lo = t * half
+
+        def square(k, total):
+            block = xg[k, lo : lo + half, :].astype(F32)
+            return total + block * block
+
+        squares = lax.fori_loop(0, NV, square, jnp.zeros((half, cols), F32))
+        r = lax.rsqrt(jnp.sum(squares, axis=-1, keepdims=True) / width + eps)
+        rcol[lo : lo + half, :] = jnp.broadcast_to(r, (half, rows))
+
+        def norm(k, carry):
+            scaled = xg[k, lo : lo + half, :].astype(F32) * rcol[lo : lo + half, 0:1]
+            begin = pl.multiple_of(k * cols, cols)
+            gain_k = xg[k, rows : rows + pads, :].astype(F32)
+            for h in range(heads):
+                line = (scaled * gain_k[8 * h : 8 * h + 1]).astype(BF16)
+                normed[h, lo : lo + half, pl.ds(begin, cols)] = line
+            return carry
+
+        lax.fori_loop(0, NV, norm, 0)
+        for h in range(heads):
+            branch = jnp.dot(normed[h, lo : lo + half, :], w[h], preferred_element_type=F32)
+            total = xg[voc, lo : lo + half, :].astype(F32) + branch
+            at = t * rows + h * half
+            hf[voc, at : at + half, :] = total.astype(BF16)
+        gather_begin(hf_at(t), hf_sem, 15 * t)
+
     for q in range(1, NY):
-        gather_row(x_at, xg_sem, 0, q)
+        gather_row(x_at(1), xg_sem, 15, q)
+    far_begin()
     ring_step(0, 1, 0)
+    for q in range(1, NY):
+        gather_row(x_at(0), xg_sem, 0, q)
+    for q in (0, 2, 1, 3):
+        gather_cross(x_at(1), xg_sem, 15, q)
+    ring_step(0, 1, 1)
     far_pass(0)
-    gather_cross(x_at, xg_sem, 0, 0)
-    gather_cross(x_at, xg_sem, 0, 2)
-    ring_step(0, 1, 1)
+    for q in (0, 2, 1, 3):
+        gather_cross(x_at(0), xg_sem, 0, q)
+    gather_end(x_at(1), xg_sem, 15)
+    ring_step(0, 2, 0)
     far_pass(1)
-    gather_cross(x_at, xg_sem, 0, 1)
-    gather_cross(x_at, xg_sem, 0, 3)
-    ring_step(0, 2, 0)
+    fetches[5].wait()
+    project(1)
+    ring_step(0, 2, 1)
+    gather_end(x_at(0), xg_sem, 0)
     ring_begin(1, 0)
-    ring_step(0, 2, 1)
-    gather_end(x_at, xg_sem, 0)
-
-    def square(k, total):
-        block = xg[k, 0:rows, :].astype(F32)
-        return total + block * block
-
-    squares = lax.fori_loop(0, NV, square, jnp.zeros((rows, cols), F32))
-    r = lax.rsqrt(jnp.sum(squares, axis=-1, keepdims=True) / width + eps)
-    r_wide = jnp.broadcast_to(r, rcol.shape)
-    rcol[...] = r_wide
-    r_line[...] = r_wide.T[0:8, :]
-
-    def norm(k, carry):
-        scaled = xg[k, 0:rows, :].astype(F32) * rcol[:, 0:1]
-        gain_k = xg[k, rows : rows + 8 * heads, :].astype(F32)
-        begin = pl.multiple_of(k * cols, cols)
-        for h in range(heads):
-            normed[h, :, pl.ds(begin, cols)] = (scaled * gain_k[8 * h : 8 * h + 1]).astype(BF16)
-        return carry
-
+    ring_step(0, 3, 0)
+    project(0)
+    r_line[...] = rcol[...].T[0:8, :]
     ring_begin(1, 1)
-    lax.fori_loop(0, NV, norm, 0)
-    ring_step(0, 3, 0)
-    fetches[5].wait()
-    for h in range(heads):
-        branch = jnp.dot(normed[h], w[h], preferred_element_type=F32)
-        hf[voc, h * rows : (h + 1) * rows, :] = (own_x + branch).astype(BF16)
-        gather_begin(hf_at(h), hf_sem, 15 * h)
-        if h == 0:
-            ring_step(1, 1, 0)
-            ring_step(0, 3, 1)
-    ring_step(1, 1, 1)
+    ring_step(0, 3, 1)
+    for q in range(1, NY):
+        gather_row(hf_at(1), hf_sem, 15, q)
+    ring_step(1, 1, 0)
+    for q in (0, 2, 1, 3):
+        gather_cross(hf_at(1), hf_sem, 15, q)
+    ring_end(0)
     for q in range(1, NY):
         gather_row(hf_at(0), hf_sem, 0, q)
-    ring_end(0)
+    ring_step(1, 1, 1)
+    for q in (0, 2, 1, 3):
+        gather_cross(hf_at(0), hf_sem, 0, q)
     ring_step(1, 2, 0)
-    for q in range(1, NY):
-        gather_row(hf_at(1), hf_sem, 15, q)
-    for q in range(NY):
-        gather_cross(hf_at(0), hf_sem, 0, q)
+    gather_end(hf_at(1), hf_sem, 15)
+    gather_end(hf_at(0), hf_sem, 0)
+
+    consume(0, 0, 3)
     ring_step(1, 2, 1)
-    gather_cross(hf_at(1), hf_sem, 15, 0)
-    gather_cross(hf_at(1), hf_sem, 15, 2)
+    consume(0, 3, 6)
     ring_step(1, 3, 0)
-    gather_cross(hf_at(1), hf_sem, 15, 1)
-    gather_cross(hf_at(1), hf_sem, 15, 3)
-    gather_end(hf_at(0), hf_sem, 0)
-    gather_end(hf_at(1), hf_sem, 15)
-
-    consume(0, 0, 5)
+    consume(0, 6, NZ)
+    consume(1, 0, 3)
     ring_step(1, 3, 1)
-    consume(0, 5, NZ)
-    consume(1, 0, 7)
+    consume(1, 3, 7)
     ring_end(1)
     consume(1, 7, NZ)
 
@@ -606,9 +624,9 @@
     grad, gain, loss = pl.pallas_call(
         kernel,
         out_shape=(
-            jax.ShapeDtypeStruct((rows, cols), F32),
-            jax.ShapeDtypeStruct((heads, cols), F32),
-            jax.ShapeDtypeStruct((8, 128), F32),
+            pltpu.VMEM((rows, cols), F32),
+            pltpu.VMEM((heads, cols), F32),
+            pltpu.VMEM((8, 128), F32),
         ),
         in_specs=[pl.BlockSpec(memory_space=pltpu.HBM)] * 6,
         out_specs=(vmem, vmem, vmem),
@@ -647,8 +665,8 @@
             pltpu.VMEM((heads, cols, rows), F32),
             pltpu.VMEM((heads, cols, rows), F32),
             dma((6,)),
-            dma((2, 15)),
-            dma((2, 15 * heads)),
+            dma((2, 30)),
+            dma((2, 30)),
             dma((2, 4)),
             dma((2, 28)),
             dma((2, 16)),

time: 136 us -> 133 us (0.978); the launches traced: 136 us -> 131 us
  local copies, waits for them, and re-layouts: 3.99 us -> 1.75 us
  Pallas kernels: 131 us -> 129 us
    pallas_call x1, Pallas kernels: 131 us -> 129 us  [per_device(): pl.pallas_call(kernel, out_shape=(pltpu.VMEM((rows, cols), F32), pltpu.VM...]
    unnamed x2, local copies, waits for them, and re-layouts: 2.8 us -> 1.23 us
where the time goes in v3:
time: 133 us; the launch traced here: 131 us
  Pallas kernels  129 us (97%)
  local copies, waits for them, and re-layouts  1.75 us (1%)
    pallas_call x1, Pallas kernels, per_device(): pl.pallas_call(kernel, out_shape=(pltpu.VMEM((rows, cols), F32), pltpu.VM...  129 us

profile of v3, /device:TPU:56, one launch (start us, length us, event | category | flops | bytes accessed | tf_op | source)
XLA Modules:
  0.0 131.1 jit_solution(3581209752350841125)
XLA Ops:
  0.6 128.7 %shard_map.85 = (f32[128,256]{1,0:T(8,128)S(1)}, f32[2,256]{1,0:T(2,128)S(1)}, f32[8,128]{1,0:T(8,128)S(1)}) custom-call(bf16[128,256]{1,0:T(8,128)(2,1)} %hidden_hbm.1, bf16[2,4096,256]{2,1,0:T(8,128)(2,1)} %w_hbm.1, bf16[2,256]{1,0:T(2,128)(2,1)} %gains_hbm.1, bf16[128,1024]{1,0:T(8,128)(2,1)} %unembed_hbm.1, s32[2,128]{1,0:T(2,128)} %targets_hbm.1, ...), custom_call_target="tpu_custom_call" | custom-call | tf_op jit(solution)/shard_map/pallas_call | solution.py:624
  129.3 0.5 slice_bitcast_fusion
  129.9 0.6 copy.12
  130.4 0.7 copy.11

commit v4 on v3

--- a/solution.py
+++ b/solution.py
@@ -153,9 +153,8 @@
 
     leg = 2 - 4 * core
 
-    def far_begin():
-        for p in range(2):
-            send(part_of(z, 0, p), relay.at[p], far_sem, p, at_level(leg))
+    def far_begin(p):
+        send(part_of(z, 0, p), relay.at[p], far_sem, p, at_level(leg))
 
     def far_pass(p):
         arrive(relay.at[p], far_sem, p)
@@ -217,10 +216,10 @@
 
         lax.fori_loop(first, last, body, 0)
 
-    for t in (1, 0):
+    for k, t in enumerate((1, 0)):
         gather_begin(x_at(t), xg_sem, 15 * t)
-    ring_begin(0, 0)
-    ring_begin(0, 1)
+        ring_begin(0, k)
+        far_begin(k)
 
     acc[...] = jnp.zeros_like(acc)
     own_x = xg[voc, 0:rows, :].astype(F32)
@@ -228,7 +227,7 @@
     for h in range(heads):
         gain_cols[h] = jnp.broadcast_to(gain_lines[h : h + 1], (rows, cols)).T
 
-    def project(t):
+    def project(t, between):
         lo = t * half
 
         def square(k, total):
@@ -248,62 +247,69 @@
                 normed[h, lo : lo + half, pl.ds(begin, cols)] = line
             return carry
 
+        between(0)
         lax.fori_loop(0, NV, norm, 0)
         for h in range(heads):
+            between(1 + h)
             branch = jnp.dot(normed[h, lo : lo + half, :], w[h], preferred_element_type=F32)
             total = xg[voc, lo : lo + half, :].astype(F32) + branch
             at = t * rows + h * half
             hf[voc, at : at + half, :] = total.astype(BF16)
         gather_begin(hf_at(t), hf_sem, 15 * t)
 
-    for q in range(1, NY):
-        gather_row(x_at(1), xg_sem, 15, q)
-    far_begin()
+    def rows_of(at, sems, base):
+        for q in range(1, NY):
+            gather_row(at, sems, base, q)
+
+    def cross_of(at, sems, base):
+        for q in (0, 2, 1, 3):
+            gather_cross(at, sems, base, q)
+
+    def first_between(k):
+        if k == 1:
+            ring_step(0, 3, 0)
+
+    def second_between(k):
+        if k == 0:
+            ring_step(0, 3, 1)
+        if k == 1:
+            ring_step(1, 1, 0)
+        if k == 2:
+            rows_of(hf_at(1), hf_sem, 15)
+
+    rows_of(x_at(1), xg_sem, 15)
     ring_step(0, 1, 0)
-    for q in range(1, NY):
-        gather_row(x_at(0), xg_sem, 0, q)
-    for q in (0, 2, 1, 3):
-        gather_cross(x_at(1), xg_sem, 15, q)
+    far_pass(0)
+    rows_of(x_at(0), xg_sem, 0)
+    cross_of(x_at(1), xg_sem, 15)
     ring_step(0, 1, 1)
-    far_pass(0)
-    for q in (0, 2, 1, 3):
-        gather_cross(x_at(0), xg_sem, 0, q)
+    far_pass(1)
+    ring_step(0, 2, 0)
+    cross_of(x_at(0), xg_sem, 0)
+    ring_begin(1, 0)
     gather_end(x_at(1), xg_sem, 15)
-    ring_step(0, 2, 0)
-    far_pass(1)
+    ring_step(0, 2, 1)
+    ring_begin(1, 1)
     fetches[5].wait()
-    project(1)
-    ring_step(0, 2, 1)
+    project(1, first_between)
     gather_end(x_at(0), xg_sem, 0)
-    ring_begin(1, 0)
-    ring_step(0, 3, 0)
-    project(0)
+    project(0, second_between)
+    ring_step(1, 1, 1)
     r_line[...] = rcol[...].T[0:8, :]
-    ring_begin(1, 1)
-    ring_step(0, 3, 1)
-    for q in range(1, NY):
-        gather_row(hf_at(1), hf_sem, 15, q)
-    ring_step(1, 1, 0)
-    for q in (0, 2, 1, 3):
-        gather_cross(hf_at(1), hf_sem, 15, q)
     ring_end(0)
-    for q in range(1, NY):
-        gather_row(hf_at(0), hf_sem, 0, q)
-    ring_step(1, 1, 1)
-    for q in (0, 2, 1, 3):
-        gather_cross(hf_at(0), hf_sem, 0, q)
+    cross_of(hf_at(1), hf_sem, 15)
     ring_step(1, 2, 0)
+    rows_of(hf_at(0), hf_sem, 0)
+    ring_step(1, 2, 1)
+    cross_of(hf_at(0), hf_sem, 0)
     gather_end(hf_at(1), hf_sem, 15)
+    ring_step(1, 3, 0)
     gather_end(hf_at(0), hf_sem, 0)
 
-    consume(0, 0, 3)
-    ring_step(1, 2, 1)
-    consume(0, 3, 6)
-    ring_step(1, 3, 0)
-    consume(0, 6, NZ)
-    consume(1, 0, 3)
+    consume(0, 0, 4)
     ring_step(1, 3, 1)
-    consume(1, 3, 7)
+    consume(0, 4, NZ)
+    consume(1, 0, 7)
     ring_end(1)
     consume(1, 7, NZ)
 
@@ -537,6 +543,14 @@
         part = jnp.sum(weighed.T, axis=0, keepdims=True)
         gain_rows[8 * h : 8 * h + 8, :] = jnp.broadcast_to(part, (8, cols))
 
+    def left_x(i):
+        for slot in range(12):
+            x_copy(i, 0, slot).wait_send()
+
+    def left_y(i):
+        for j in range(1, NY):
+            y_copy(i, lax.rem(y + j, NY)).wait_send()
+
     loop4(across_heads)
     loop4(near_heads)
     loop4(last_heads)
@@ -549,15 +563,32 @@
     norm_begin(0)
     column(1)
     norm_pass(0)
+    for copy in pending:
+        copy.wait_send()
+    pending.clear()
+    left_x(0)
+    left_y(0)
+    left_x(1)
     head_done(1)
     norm_begin(1)
     column(2)
     norm_pass(1)
+    left_y(1)
+    left_x(2)
     norm_done(0)
     gain_done(0)
     column(3)
     norm_done(1)
 
+    for h in range(1, heads):
+        gain_done(h)
+    line = lax.broadcasted_iota(jnp.int32, (8, cols), 0)
+    packed = jnp.where(line == heads, lossrow[...], 0.0)
+    for h in range(heads):
+        packed = packed + jnp.where(line == h, gain_rows[8 * h : 8 * h + 8, :], 0.0)
+    gain_p[0] = packed
+    for k in (2, 3, 1):
+        send(gain_p.at[0], gain_p.at[k], gain_sem, k - 1, at_pair(k))
     scaled = jnp.zeros((cols, rows), F32)
     for h in range(heads):
         scaled = scaled + gain_cols[h] * norm_grad[h]
@@ -565,15 +596,6 @@
     dot_x[0] = jnp.broadcast_to(dots, (8, rows))
     for j in range(1, NX):
         send(dot_x.at[0], dot_x.at[j], dot_sem, j - 1, at_x(j))
-    for h in range(1, heads):
-        gain_done(h)
-    line = lax.broadcasted_iota(jnp.int32, (8, cols), 0)
-    packed = jnp.where(line == heads, lossrow[...], 0.0)
-    for h in range(heads):
-        packed = packed + jnp.where(line == h, gain_rows[8 * h : 8 * h + 8, :], 0.0)
-    gain_p[0] = packed
-    for k in range(1, 4):
-        send(gain_p.at[0], gain_p.at[k], gain_sem, k - 1, at_pair(k))
     for j in range(1, NX):
         arrive(dot_x.at[j], dot_sem, j - 1)
     dot_y[0] = dot_x[0] + dot_x[1] + dot_x[2] + dot_x[3]
@@ -606,11 +628,9 @@
     loss_out[...] = losses
     for copy in pending:
         copy.wait_send()
-    for i in range(2 * heads):
-        for slot in range(12):
-            x_copy(i, 0, slot).wait_send()
-        for j in range(1, NY):
-            y_copy(i, lax.rem(y + j, NY)).wait_send()
+    left_y(2)
+    left_x(3)
+    left_y(3)
 
 
 def per_device(hidden, head_weight, gains, unembed, targets, loss_weights):

time: 133 us -> 131 us (0.985); the launches traced: 131 us -> 131 us
  no operation moved by 1% of the time
where the time goes in v4:
time: 131 us
  Pallas kernels  129 us (98%)
  local copies, waits for them, and re-layouts  1.75 us (1%)
    pallas_call x1, Pallas kernels, per_device(): pl.pallas_call(kernel, out_shape=(pltpu.VMEM((rows, cols), F32), pltpu.VM...  129 us

profile of v4, /device:TPU:56, one launch (start us, length us, event | category | flops | bytes accessed | tf_op | source)
XLA Modules:
  0.0 131.0 jit_solution(13434331100986395368)
XLA Ops:
  0.6 128.6 %shard_map.85 = (f32[128,256]{1,0:T(8,128)S(1)}, f32[2,256]{1,0:T(2,128)S(1)}, f32[8,128]{1,0:T(8,128)S(1)}) custom-call(bf16[128,256]{1,0:T(8,128)(2,1)} %hidden_hbm.1, bf16[2,4096,256]{2,1,0:T(8,128)(2,1)} %w_hbm.1, bf16[2,256]{1,0:T(2,128)(2,1)} %gains_hbm.1, bf16[128,1024]{1,0:T(8,128)(2,1)} %unembed_hbm.1, s32[2,128]{1,0:T(2,128)} %targets_hbm.1, ...), custom_call_target="tpu_custom_call" | custom-call | tf_op jit(solution)/shard_map/pallas_call | solution.py:644
  129.2 0.5 slice_bitcast_fusion
  129.7 0.6 copy.12
  130.3 0.7 copy.11

commit v5 on v4

--- a/solution.py
+++ b/solution.py
@@ -195,26 +195,23 @@
             ring_arrive(zz, e, way, 4, way)
         share(e, 7, zz)
 
-    def consume(e, first, last):
+    def consume(e, slabs):
         far_e = 1 - far if e else far
-
-        def body(k, carry):
-            dist = lax.div(k + 1, 2)
-            zz = lax.rem(z + NZ + dist * (1 - 2 * lax.rem(k, 2)), NZ)
+        left_parts, right_parts = [], []
+        for k in slabs:
+            zz = z_at((k + 1) // 2 * (1 - 2 * (k % 2)))
             arrive(slab(zz, e, False), share_sem, e * NZ + k)
             block = zz * NFAR + far_e
-            begin = pl.multiple_of(block * cols, cols)
             lines = [
                 hf[block, t * rows + h * half : t * rows + (h + 1) * half, :]
                 for h in range(heads) for t in range(2)
             ]
-            acc[...] += jnp.dot(
-                jnp.concatenate(lines, axis=0), table[pl.ds(begin, cols), :],
-                preferred_element_type=F32,
-            )
-            return carry
-
-        lax.fori_loop(first, last, body, 0)
+            left_parts.append(jnp.concatenate(lines, axis=0))
+            right_parts.append(table[pl.ds(pl.multiple_of(block * cols, cols), cols), :])
+        acc[...] += jnp.dot(
+            jnp.concatenate(left_parts, axis=1), jnp.concatenate(right_parts, axis=0),
+            preferred_element_type=F32,
+        )
 
     for k, t in enumerate((1, 0)):
         gather_begin(x_at(t), xg_sem, 15 * t)
@@ -306,12 +303,13 @@
     ring_step(1, 3, 0)
     gather_end(hf_at(0), hf_sem, 0)
 
-    consume(0, 0, 4)
+    consume(0, (0, 1, 2, 3))
     ring_step(1, 3, 1)
-    consume(0, 4, NZ)
-    consume(1, 0, 7)
+    consume(0, (4, 5, 6, 7))
+    consume(1, (0, 1, 2))
+    consume(1, (3, 4, 5, 6))
     ring_end(1)
-    consume(1, 7, NZ)
+    consume(1, (7,))
 
     step = 128
     ids = jnp.concatenate([targets[h : h + 1, :] for h in range(heads)], axis=1) - voc * voc_dev
@@ -387,8 +385,10 @@
         out = jnp.dot(table[block_rows(way, yb), :], up[...], preferred_element_type=F32)
         return [out[:, h * rows : (h + 1) * rows] for h in range(heads)]
 
-    def norm_part(h, way, yb):
-        return jnp.dot(w[h, block_rows(way, yb), :], low[h], preferred_element_type=F32)
+    def norm_parts(h, blocks):
+        lines = [w[h, block_rows(way, yb), :] for way, yb in blocks]
+        out = jnp.dot(jnp.concatenate(lines, axis=0), low[h], preferred_element_type=F32)
+        return [out[k * cols : (k + 1) * cols] for k in range(len(blocks))]
 
     def across_of(n):
         way, b = lax.rem(n, 2), lax.div(n, 2)
@@ -505,35 +505,23 @@
 
     def norm_begin(h):
         i = heads + h
-
-        def across(n):
-            way, yb, slot = across_of(n)
-            rs_send[i, slot] = norm_part(h, 2, yb).astype(BF16)
-            x_copy(i, way, slot).start()
-
-        def near(n):
-            way, yb, slot = near_of(n)
-            rs_send[i, slot] = norm_part(h, 1 + 2 * way, yb).astype(BF16)
-            x_copy(i, way, slot).start()
-
-        loop4(across)
-        loop4(near)
+        for stage, shift in (((0, 0, 0), (1, 2, 2), (0, 1, 1), (1, 3, 3)), 1), (
+            ((0, 2, 6), (1, 0, 8), (0, 3, 7), (1, 1, 9)), 0
+        ):
+            blocks = [(2 if shift else 1 + 2 * way, yb) for way, yb, slot in stage]
+            for (way, yb, slot), part in zip(stage, norm_parts(h, blocks)):
+                rs_send[i, slot] = part.astype(BF16)
+                x_copy(i, way, slot).start()
 
     def norm_pass(h):
         i = heads + h
-
-        def own(n):
-            rs_own[i, n] = norm_part(h, 0, n)
-
-        def last(n):
-            way, yb, slot = last_of(n)
-            part = norm_part(h, 1 + 2 * way, yb)
+        stage = ((0, 0, 4), (1, 2, 10), (0, 1, 5), (1, 3, 11))
+        for (way, yb, slot), part in zip(stage, norm_parts(h, [(1 + 2 * way, yb) for way, yb, slot in stage])):
             x_arrive(i, yb)
             rs_send[i, slot] = (part + rs_in[i, yb].astype(F32)).astype(BF16)
             x_copy(i, way, slot).start()
-
-        loop4(own)
-        loop4(last)
+        for n, part in enumerate(norm_parts(h, [(0, n) for n in range(4)])):
+            rs_own[i, n] = part
 
     def norm_done(h):
         norm_grad[h] = finish(heads + h)

time: 131 us -> 128 us (0.977)
  Pallas kernels: 129 us -> 125 us
    pallas_call x1, Pallas kernels: 129 us -> 125 us  [per_device(): pl.pallas_call(kernel, out_shape=(pltpu.VMEM((rows, cols), F32), pltpu.VM...]
where the time goes in v5:
time: 128 us
  Pallas kernels  125 us (98%)
  local copies, waits for them, and re-layouts  1.75 us (1%)
    pallas_call x1, Pallas kernels, per_device(): pl.pallas_call(kernel, out_shape=(pltpu.VMEM((rows, cols), F32), pltpu.VM...  125 us

profile of v5, /device:TPU:56, one launch (start us, length us, event | category | flops | bytes accessed | tf_op | source)
XLA Modules:
  0.0 127.9 jit_solution(2252346081269640484)
XLA Ops:
  0.6 125.5 %shard_map.85 = (f32[128,256]{1,0:T(8,128)S(1)}, f32[2,256]{1,0:T(2,128)S(1)}, f32[8,128]{1,0:T(8,128)S(1)}) custom-call(bf16[128,256]{1,0:T(8,128)(2,1)} %hidden_hbm.1, bf16[2,4096,256]{2,1,0:T(8,128)(2,1)} %w_hbm.1, bf16[2,256]{1,0:T(2,128)(2,1)} %gains_hbm.1, bf16[128,1024]{1,0:T(8,128)(2,1)} %unembed_hbm.1, s32[2,128]{1,0:T(2,128)} %targets_hbm.1, ...), custom_call_target="tpu_custom_call" | custom-call | tf_op jit(solution)/shard_map/pallas_call | solution.py:632
  126.1 0.5 slice_bitcast_fusion
  126.6 0.6 copy.12
  127.2 0.7 copy.11

commit v6 on v5

--- a/solution.py
+++ b/solution.py
@@ -119,13 +119,19 @@
         arrive(at(slot), sems, base + k)
         send(at(slot), at(slot), sems, base + 11 + q, to)
 
-    def gather_end(at, sems, base):
+    def gather_near(at, sems, base):
         for q in (2, 3):
             arrive(at(row(q) + left), sems, base + 3 + q)
         for q in (0, 1):
             arrive(at(row(q) + right), sems, base + 7 + q)
+
+    def gather_over(at, sems, base):
         for q in range(NY):
             arrive(at(row(q) + over), sems, base + 11 + q)
+
+    def gather_end(at, sems, base):
+        gather_near(at, sems, base)
+        gather_over(at, sems, base)
 
     half = rows // 2
     pads = 8 * heads
@@ -195,30 +201,36 @@
             ring_arrive(zz, e, way, 4, way)
         share(e, 7, zz)
 
-    def consume(e, slabs):
-        far_e = 1 - far if e else far
+    def logit_blocks(blocks):
         left_parts, right_parts = [], []
-        for k in slabs:
-            zz = z_at((k + 1) // 2 * (1 - 2 * (k % 2)))
-            arrive(slab(zz, e, False), share_sem, e * NZ + k)
-            block = zz * NFAR + far_e
+        for block in blocks:
             lines = [
                 hf[block, t * rows + h * half : t * rows + (h + 1) * half, :]
                 for h in range(heads) for t in range(2)
             ]
             left_parts.append(jnp.concatenate(lines, axis=0))
             right_parts.append(table[pl.ds(pl.multiple_of(block * cols, cols), cols), :])
-        acc[...] += jnp.dot(
+        return jnp.dot(
             jnp.concatenate(left_parts, axis=1), jnp.concatenate(right_parts, axis=0),
             preferred_element_type=F32,
         )
+
+    def slab_at(k):
+        return z_at((k + 1) // 2 * (1 - 2 * (k % 2)))
+
+    def consume(slabs):
+        blocks = []
+        for k in slabs:
+            zz = slab_at(k)
+            arrive(slab(zz, 1, False), share_sem, NZ + k)
+            blocks.append(zz * NFAR + 1 - far)
+        acc[...] += logit_blocks(blocks)
 
     for k, t in enumerate((1, 0)):
         gather_begin(x_at(t), xg_sem, 15 * t)
         ring_begin(0, k)
         far_begin(k)
 
-    acc[...] = jnp.zeros_like(acc)
     own_x = xg[voc, 0:rows, :].astype(F32)
     x_t[...] = own_x.T
     for h in range(heads):
@@ -299,17 +311,23 @@
     rows_of(hf_at(0), hf_sem, 0)
     ring_step(1, 2, 1)
     cross_of(hf_at(0), hf_sem, 0)
-    gather_end(hf_at(1), hf_sem, 15)
     ring_step(1, 3, 0)
-    gather_end(hf_at(0), hf_sem, 0)
-
-    consume(0, (0, 1, 2, 3))
+    gather_near(hf_at(1), hf_sem, 15)
+    gather_near(hf_at(0), hf_sem, 0)
+
+    for k in range(NZ):
+        arrive(slab(slab_at(k), 0, False), share_sem, k)
+    column_1 = lax.rem(x + NX - lax.rem(x + far, 2), NX)
+    column_2 = lax.rem(column_1 + 2, NX)
+    acc[...] = logit_blocks([yb * NX + column_1 for yb in range(NY)])
     ring_step(1, 3, 1)
-    consume(0, (4, 5, 6, 7))
-    consume(1, (0, 1, 2))
-    consume(1, (3, 4, 5, 6))
+    gather_over(hf_at(1), hf_sem, 15)
+    gather_over(hf_at(0), hf_sem, 0)
+    acc[...] += logit_blocks([yb * NX + column_2 for yb in range(NY)])
+    consume((0, 1, 2))
+    consume((3, 4, 5, 6))
     ring_end(1)
-    consume(1, (7,))
+    consume((7,))
 
     step = 128
     ids = jnp.concatenate([targets[h : h + 1, :] for h in range(heads)], axis=1) - voc * voc_dev
@@ -381,9 +399,13 @@
         block = yb * NX + lax.rem(x + way, NX)
         return pl.ds(pl.multiple_of(block * cols, cols), cols)
 
-    def head_part(way, yb):
-        out = jnp.dot(table[block_rows(way, yb), :], up[...], preferred_element_type=F32)
-        return [out[:, h * rows : (h + 1) * rows] for h in range(heads)]
+    def head_parts(blocks):
+        lines = [table[block_rows(way, yb), :] for way, yb in blocks]
+        out = jnp.dot(jnp.concatenate(lines, axis=0), up[...], preferred_element_type=F32)
+        return [
+            [out[k * cols : (k + 1) * cols, h * rows : (h + 1) * rows] for h in range(heads)]
+            for k in range(len(blocks))
+        ]
 
     def norm_parts(h, blocks):
         lines = [w[h, block_rows(way, yb), :] for way, yb in blocks]
@@ -456,26 +478,27 @@
             total = total + ys_recv[i, peer].astype(F32)
         return total
 
-    def across_heads(n):
-        way, yb, slot = across_of(n)
-        for h, part in enumerate(head_part(2, yb)):
-            rs_send[h, slot] = part.astype(BF16)
-        x_copy(0, way, slot).start()
-
-    def near_heads(n):
-        way, yb, slot = near_of(n)
-        for h, part in enumerate(head_part(1 + 2 * way, yb)):
-            rs_send[h, slot] = part.astype(BF16)
-        x_copy(0, way, slot).start()
-
-    def last_heads(n):
-        way, yb, slot = last_of(n)
-        for h, part in enumerate(head_part(1 + 2 * way, yb)):
-            rs_part[h, yb] = part
-
-    def own_heads(n):
-        for h, part in enumerate(head_part(0, n)):
-            rs_own[h, n] = part
+    def begin_heads(stage):
+        parts = head_parts([(step, yb) for step, way, yb, slot in stage])
+        for (step, way, yb, slot), part in zip(stage, parts):
+            for h in range(heads):
+                rs_send[h, slot] = part[h].astype(BF16)
+            x_copy(0, way, slot).start()
+
+    def last_heads():
+        stage = ((0, 0, 4), (1, 2, 10), (0, 1, 5), (1, 3, 11))
+        parts = head_parts([(1 + 2 * way, yb) for way, yb, slot in stage])
+        for (way, yb, slot), part in zip(stage, parts):
+            for h in range(1, heads):
+                rs_part[h, yb] = part[h]
+            x_arrive(0, yb)
+            rs_send[0, slot] = (part[0] + rs_in[0, yb].astype(F32)).astype(BF16)
+            x_copy(0, way, slot).start()
+
+    def own_heads():
+        for n, part in enumerate(head_parts([(0, n) for n in range(4)])):
+            for h in range(heads):
+                rs_own[h, n] = part[h]
 
     def send_heads(h):
         def across(n):
@@ -539,12 +562,13 @@
         for j in range(1, NY):
             y_copy(i, lax.rem(y + j, NY)).wait_send()
 
-    loop4(across_heads)
-    loop4(near_heads)
-    loop4(last_heads)
-    pass_heads(0)
+    begin_heads(((2, 0, 0, 0), (2, 1, 2, 2)))
+    begin_heads(((2, 0, 1, 1), (2, 1, 3, 3)))
+    begin_heads(((1, 0, 2, 6), (3, 1, 0, 8)))
+    begin_heads(((1, 0, 3, 7), (3, 1, 1, 9)))
+    last_heads()
     send_heads(1)
-    loop4(own_heads)
+    own_heads()
     column(0)
     pass_heads(1)
     head_done(0)

time: 128 us -> 129 us (level)
  no operation moved by 1% of the time
where the time goes in v6:
time: 129 us; the launch traced here: 128 us
  Pallas kernels  126 us (98%)
  local copies, waits for them, and re-layouts  1.75 us (1%)
    pallas_call x1, Pallas kernels, per_device(): pl.pallas_call(kernel, out_shape=(pltpu.VMEM((rows, cols), F32), pltpu.VM...  126 us

profile of v6, /device:TPU:56, one launch (start us, length us, event | category | flops | bytes accessed | tf_op | source)
XLA Modules:
  0.0 128.4 jit_solution(9162829085655932743)
XLA Ops:
  0.6 126.0 %shard_map.85 = (f32[128,256]{1,0:T(8,128)S(1)}, f32[2,256]{1,0:T(2,128)S(1)}, f32[8,128]{1,0:T(8,128)S(1)}) custom-call(bf16[128,256]{1,0:T(8,128)(2,1)} %hidden_hbm.1, bf16[2,4096,256]{2,1,0:T(8,128)(2,1)} %w_hbm.1, bf16[2,256]{1,0:T(2,128)(2,1)} %gains_hbm.1, bf16[128,1024]{1,0:T(8,128)(2,1)} %unembed_hbm.1, s32[2,128]{1,0:T(2,128)} %targets_hbm.1, ...), custom_call_target="tpu_custom_call" | custom-call | tf_op jit(solution)/shard_map/pallas_call | solution.py:656
  126.7 0.5 slice_bitcast_fusion
  127.2 0.6 copy.12
  127.7 0.7 copy.11
